TPU v7x, 512 devices: a whole 4x8x8 slice. The times are simulated.
512 devices in a mesh: wide: 32 (over x, y), narrow: 16 (over z, core).
Axes of the slice: x: 4, y: 8, z: 8, core: 2. Of those that a mesh axis runs over, the one named last changes fastest.
Arguments:
- student_feats: bfloat16 [1024, 512], P(('wide', 'narrow')), may hold values from -8 to 8
- teacher_feats: bfloat16 [1024, 512], P(('wide', 'narrow')), may hold values from -8 to 8
- prototypes: bfloat16 [262144, 512], P(('wide', 'narrow')), may hold values from -8 to 8
Outputs:
- student_grad: float32 [1024, 512], P(('wide', 'narrow'))
- proto_grad: float32 [262144, 512], P(('wide', 'narrow'))
All inputs are finite; a program needn't handle non-finite values.
Results may differ from a plain program's by a relative error of at most 0.0006.
The roundings to bfloat16 on the way count: a program that leaves them out, or rounds other values in their place, can miss the bound.
Values may be sent and summed in bfloat16 or wider, within the bound.
A program may use at most 64 MiB of HBM per device.

v0:
```python
import jax
import jax.numpy as jnp
from jax import lax
from jax.sharding import Mesh
from jax.sharding import PartitionSpec as P

SINK_ITERS = 3
WIDE_NARROW = ("wide_0", "wide_1", "narrow_0", "narrow_1")
NARROW = ("narrow_0", "narrow_1")
WIDE = ("wide_0", "wide_1")


epsilon = 1e-06
teacher_temp = 0.07
student_temp = 0.1
loss_scale = 1.0


def from_everyone(shard, axis):
    copies = jnp.broadcast_to(shard, (lax.axis_size(axis), *shard.shape))
    return lax.all_to_all(copies, axis, split_axis=0, concat_axis=0, tiled=True)


def taken_together(shard, axis):
    return from_everyone(shard, axis).sum(axis=0)


def one_axis_at_a_time(shard, axes):
    far, near = axes
    nearer = taken_together(shard, near)
    return taken_together(nearer, far)


def in_order(parts, dim):
    shape = list(parts.shape[1:])
    shape[dim] *= parts.shape[0]
    return jnp.moveaxis(parts, 0, dim).reshape(shape)


def gathered_by_axis(shard, axes, dim):
    far, near = axes
    initial = from_everyone(shard, far)
    parts = jnp.swapaxes(from_everyone(initial, near), 0, 1)
    return in_order(parts.reshape(-1, *shard.shape), dim)


def packed_total(arrays, axis):
    vector, at, gathered = (jnp.concatenate([a.reshape(-1) for a in arrays]), 0, [])
    total = one_axis_at_a_time(vector, axis)
    for a in arrays:
        gathered.append(total[at : at + a.size].reshape(a.shape))
        at += a.size
    return tuple(gathered)


def split_up(shard, dim, peers):
    before, after = (shard.shape[:dim], shard.shape[dim + 1 :])
    return jnp.moveaxis(shard.reshape(*before, peers, -1, *after), dim, 0)


def sum_at_owner(shard, axis, dim):
    parts = split_up(shard, dim, lax.axis_size(axis))
    arrived = lax.all_to_all(parts, axis, split_axis=0, concat_axis=0, tiled=True)
    return arrived.sum(axis=0)


def unit_rows(values):
    widened = values.astype(jnp.float32)
    inverse = lax.rsqrt(jnp.sum(widened * widened, axis=1, keepdims=True) + epsilon)
    return (widened * inverse, inverse)


def row_mass(partial_value):
    return one_axis_at_a_time(partial_value, (("wide_0", "wide_1"), ("narrow_0", "narrow_1")))


def on_device(student_feats, teacher_feats, prototypes):
    student_unit, student_inv = unit_rows(student_feats)
    teacher_unit = unit_rows(teacher_feats)[0]
    proto_unit, proto_inv = unit_rows(prototypes)
    proto_hat = proto_unit.astype(jnp.bfloat16)
    paired = jnp.stack([student_unit, teacher_unit]).astype(jnp.bfloat16)
    gathered = gathered_by_axis(paired, (("wide_0", "wide_1"), ("narrow_0", "narrow_1")), 1)
    logits = jnp.einsum("srd,pd->srp", gathered, proto_hat, preferred_element_type=jnp.float32)
    exp_student = jnp.exp(logits[0] / student_temp)
    exp_teacher = jnp.exp(logits[1] / teacher_temp)
    student_part = jnp.sum(exp_student, axis=1)
    col_scale = 1.0 / jnp.sum(exp_teacher, axis=0)
    teacher_part = jnp.sum(exp_teacher * col_scale[None, :], axis=1)
    teacher_total, student_total = packed_total(
        (teacher_part, student_part), (("wide_0", "wide_1"), ("narrow_0", "narrow_1"))
    )
    row_scale = 1.0 / teacher_total
    for sweep in range(SINK_ITERS - 1):
        col_scale = 1.0 / jnp.sum(exp_teacher * row_scale[:, None], axis=0)
        row_scale = 1.0 / row_mass(jnp.sum(exp_teacher * col_scale[None, :], axis=1))
    target = row_scale[:, None] * exp_teacher * col_scale[None, :]
    student_prob = exp_student / student_total[:, None]
    grad_logits = (loss_scale * (student_prob - target) / student_temp).astype(jnp.bfloat16)
    proto_step = jnp.einsum(
        "bp,bd->pd", grad_logits, gathered[0], preferred_element_type=jnp.float32
    )
    proto_grad = (
        proto_step - proto_unit * jnp.sum(proto_unit * proto_step, axis=1, keepdims=True)
    ) * proto_inv
    outer = sum_at_owner(
        jnp.einsum("bp,pd->bd", grad_logits, proto_hat, preferred_element_type=jnp.float32), WIDE, 0
    )
    row_step = sum_at_owner(outer, NARROW, 0)
    student_grad = (
        row_step - student_unit * jnp.sum(student_unit * row_step, axis=1, keepdims=True)
    ) * student_inv
    return (student_grad, proto_grad)


def solution(mesh):
    torus = Mesh(mesh.devices.reshape(4, 8, 8, 2), ("wide_0", "wide_1", "narrow_0", "narrow_1"))
    placed = (P(WIDE_NARROW, None), P(WIDE_NARROW, None), P(WIDE_NARROW, None))
    return jax.shard_map(
        on_device,
        mesh=torus,
        in_specs=placed,
        out_specs=(P(WIDE_NARROW, None), P(WIDE_NARROW, None)),
        check_vma=False,
    )
```

profile of v0, /device:TPU:1, one launch (start us, length us, event | category | flops | bytes accessed | tf_op | source)
XLA Modules:
  0.0 268.1 jit_solution(7693124704500384842)
XLA Ops:
  0.6 0.8 fusion.28
  1.4 0.8 fusion.27
  2.3 0.8 fusion.30
  3.1 19.5 %all_to_all.56 = bf16[32,2,2,512]{3,2,1,0:T(2,128)(2,1)S(1)} all-to-all(bf16[32,2,2,512]{3,2,1,0:T(2,128)(2,1)S(1)} %broadcast_in_dim.16), channel_id=1, replica_groups=mesh['wide_0'=4,'wide_1'=8,'narrow_0'=8,'narrow_1'=2] {'wide_0','wide_1'}, dimensions={0} | all-to-all | bytes 262144 | tf_op jit(solution)/shard_map/all_to_all | solution.py:21
  22.6 0.1 copy.46
  22.7 3.2 %broadcast_in_dim.17 = bf16[16,32,2,2,512]{4,3,1,2,0:T(2,128)(2,1)} broadcast(bf16[32,2,2,512]{3,2,0,1:T(2,128)(2,1)S(1)} %copy.46), dimensions={1,2,3,4} | broadcast | bytes 2228224 | tf_op jit(solution)/shard_map/broadcast_in_dim | solution.py:20
  25.9 12.5 %all-to-all-start.1 = ((bf16[16,32,2,2,512]{4,3,1,2,0:T(2,128)(2,1)}), bf16[16,32,2,2,512]{4,3,1,2,0:T(2,128)(2,1)}, u32[]{:S(2)}, u32[]{:S(2)}) async-start(bf16[16,32,2,2,512]{4,3,1,2,0:T(2,128)(2,1)} %broadcast_in_dim.17), calls=%async_computation.1 | async-start | bytes 4194304 | tf_op jit(solution)/shard_map/all_to_all | solution.py:21
  38.4 0.2 copy.49
  38.6 0.2 fusion.13
  38.8 48.7 %all-to-all-done.1 = bf16[16,32,2,2,512]{4,3,1,2,0:T(2,128)(2,1)} async-done(((bf16[16,32,2,2,512]{4,3,1,2,0:T(2,128)(2,1)}), bf16[16,32,2,2,512]{4,3,1,2,0:T(2,128)(2,1)}, u32[]{:S(2)}, u32[]{:S(2)}) %all-to-all-start.1) | async-done | bytes 2097184 | tf_op jit(solution)/shard_map/all_to_all | solution.py:21
  87.4 2.8 %copy.47 = bf16[16,32,2,2,512]{4,0,1,3,2:T(8,128)(2,1)S(1)} copy(bf16[16,32,2,2,512]{4,3,1,2,0:T(2,128)(2,1)} %all-to-all-done.1) | data formatting | bytes 4194304 | tf_op jit(solution)/shard_map/all_to_all | solution.py:21
  90.2 3.5 %copy.48 = bf16[2,512,2,512]{3,2,1,0:T(2,128)(2,1)} copy(bf16[2,512,2,512]{3,1,2,0:T(8,128)(2,1)S(1)} %bitcast.39) | data formatting | bytes 4194304 | tf_op jit(solution)/shard_map/transpose | solution.py:37
  93.7 4.1 %reshape.135 = bf16[2,1024,512]{2,1,0:T(8,128)(2,1)} reshape(bf16[2,512,2,512]{3,2,1,0:T(2,128)(2,1)} %copy.48) | data formatting | bytes 4194304 | tf_op jit(solution)/shard_map/reshape | solution.py:37
  97.8 2.9 %fusion.19 = f32[2,1024,512]{2,1,0:T(8,128)S(1)} fusion(bf16[2,1024,512]{2,1,0:T(8,128)(2,1)} %reshape.135, bf16[512,512]{0,1:T(8,128)(2,1)S(1)} %copy.49, f32[512]{0:T(512)S(1)} %add_rsqrt_fusion), kind=kOutput, calls=%fused_computation.29 | convolution fusion | flops 1074528256 | bytes 6817792 | tf_op jit(solution)/shard_map/srd,pd->srp/dot_general | solution.py:84
  100.7 2.6 fusion.37
  103.3 0.7 copy-done
  103.9 0.4 fusion.2
  104.4 13.9 %all_to_all.57 = f32[16,1,2048]{2,1,0:T(1,128)S(1)} all-to-all(f32[16,1,2048]{2,1,0:T(1,128)S(1)} %broadcast_in_dim.18), channel_id=1, replica_groups=mesh['wide_0'=4,'wide_1'=8,'narrow_0'=8,'narrow_1'=2] {'narrow_0','narro..., dimensions={0} | all-to-all | bytes 262144 | tf_op jit(solution)/shard_map/all_to_all | solution.py:21
  118.4 0.1 reduce_sum.186
  118.5 0.1 broadcast_in_dim.19
  118.6 14.0 %all_to_all.58 = f32[32,1,2048]{2,1,0:T(1,128)S(1)} all-to-all(f32[32,1,2048]{2,1,0:T(1,128)S(1)} %broadcast_in_dim.19), channel_id=1, replica_groups=mesh['wide_0'=4,'wide_1'=8,'narrow_0'=8,'narrow_1'=2] {'wide_0','wide_1'}, dimensions={0} | all-to-all | bytes 524288 | tf_op jit(solution)/shard_map/all_to_all | solution.py:21
  132.6 0.2 reduce_sum.187
  132.8 2.0 fusion.3
  134.8 2.0 fusion.4
  136.8 12.5 %all_to_all.59 = f32[16,1,1024]{2,1,0:T(1,128)S(1)} all-to-all(f32[16,1,1024]{2,1,0:T(1,128)S(1)} %broadcast_in_dim.20), channel_id=1, replica_groups=mesh['wide_0'=4,'wide_1'=8,'narrow_0'=8,'narrow_1'=2] {'narrow_0','narro..., dimensions={0} | all-to-all | bytes 131072 | tf_op jit(solution)/shard_map/all_to_all | solution.py:21
  149.4 13.5 %all_to_all.60 = f32[32,1,1024]{2,1,0:T(1,128)S(1)} all-to-all(f32[32,1,1024]{2,1,0:T(1,128)S(1)} %broadcast_in_dim.42), channel_id=1, replica_groups=mesh['wide_0'=4,'wide_1'=8,'narrow_0'=8,'narrow_1'=2] {'wide_0','wide_1'}, dimensions={0} | all-to-all | bytes 262144 | tf_op jit(solution)/shard_map/all_to_all | solution.py:21
  163.0 0.1 reduce_sum.191
  163.1 2.0 fusion.5
  165.0 2.0 fusion.6
  167.1 12.3 %all_to_all.61 = f32[16,1,1024]{2,1,0:T(1,128)S(1)} all-to-all(f32[16,1,1024]{2,1,0:T(1,128)S(1)} %broadcast_in_dim.43), channel_id=1, replica_groups=mesh['wide_0'=4,'wide_1'=8,'narrow_0'=8,'narrow_1'=2] {'narrow_0','narro..., dimensions={0} | all-to-all | bytes 131072 | tf_op jit(solution)/shard_map/all_to_all | solution.py:21
  179.5 0.7 broadcast_in_dim.44
  180.2 3.9 %all-to-all-start.7 = ((f32[32,1,1024]{2,1,0:T(1,128)}), f32[32,1,1024]{2,1,0:T(1,128)S(1)}, u32[]{:S(2)}, u32[]{:S(2)}) async-start(f32[32,1,1024]{2,1,0:T(1,128)} %broadcast_in_dim.44), calls=%async_computation.7 | async-start | bytes 262144 | tf_op jit(solution)/shard_map/all_to_all | solution.py:21
  184.2 9.1 %all-to-all-done.7 = f32[32,1,1024]{2,1,0:T(1,128)S(1)} async-done(((f32[32,1,1024]{2,1,0:T(1,128)}), f32[32,1,1024]{2,1,0:T(1,128)S(1)}, u32[]{:S(2)}, u32[]{:S(2)}) %all-to-all-start.7) | async-done | bytes 131104 | tf_op jit(solution)/shard_map/all_to_all | solution.py:21
  193.2 0.1 reduce_sum.195
  193.4 4.3 %fusion.16 = f32[32,32,512]{2,1,0:T(8,128)} fusion(f32[32,32,512]{2,1,0:T(8,128)} %bitcast.41, f32[32,32,512]{2,1,0:T(8,128)} %bitcast.42, f32[512]{0:T(512)S(1)} %broadcast_divide_fusion.2, f32[32,32]{1,0:T(8,128)S(1)} %div.84, f32[32,32]{1,0:T(8,128)S(1)} %div.76, bf16[512,512]{0,1:T(8,128)(2,1)S(1)} %copy.49, f32[512]{0:T(512)S(1)} %add_rsqrt_fusion), kind=kOutput, calls=%fused_computation.27 | convolution fusion | flops 540803072 | bytes 6828032 | tf_op jit(solution)/shard_map/bp,pd->bd/dot_general | solution.py:107
  197.7 4.8 %all-to-all-start.8 = ((f32[32,32,512]{2,1,0:T(8,128)}), f32[32,32,512]{2,1,0:T(8,128)}, u32[]{:S(2)}, u32[]{:S(2)}) async-start(f32[32,32,512]{2,1,0:T(8,128)} %fusion.16), calls=%async_computation.8 | async-start | bytes 4194304 | tf_op jit(solution)/shard_map/all_to_all | solution.py:63
  202.6 1.1 copy.59
  203.7 1.2 squeeze.2
  204.9 3.8 %fusion.10 = (f32[512]{0:T(512)S(1)}, f32[512,512]{0,1:T(8,128)S(1)}) fusion(bf16[512,512]{0,1:T(8,128)(2,1)S(1)} %copy.49, f32[512]{0:T(512)S(1)} %add_rsqrt_fusion, bf16[1024,512]{1,0:T(8,128)(2,1)} %squeeze.2, f32[512]{0:T(512)S(1)} %broadcast_divide_fusion.2, f32[1024]{0:T(1024)S(1)} %broadcast_divide_fusion, f32[1024]{0:T(1024)S(1)} %get-tuple-element.20, ...), kind=kOutput, calls=%fused_computation.21 | convolution fusion | flops 542113280 | bytes 6830080 | tf_op jit(solution)/shard_map/bp,bd->pd/dot_general | solution.py:100
  208.7 43.2 %all-to-all-done.8 = f32[32,32,512]{2,1,0:T(8,128)} async-done(((f32[32,32,512]{2,1,0:T(8,128)}), f32[32,32,512]{2,1,0:T(8,128)}, u32[]{:S(2)}, u32[]{:S(2)}) %all-to-all-start.8) | async-done | bytes 2097184 | tf_op jit(solution)/shard_map/all_to_all | solution.py:63
  251.9 1.7 reduce_sum.196
  253.7 0.7 reshape.136
  254.3 5.1 %all-to-all-start.9 = ((f32[16,2,512]{2,1,0:T(2,128)}), f32[16,2,512]{2,1,0:T(2,128)S(1)}, u32[]{:S(2)}, u32[]{:S(2)}) async-start(f32[16,2,512]{2,1,0:T(2,128)} %reshape.136), calls=%async_computation.9 | async-start | bytes 131072 | tf_op jit(solution)/shard_map/all_to_all | solution.py:63
  259.4 0.2 fusion.12
  259.6 1.3 copy.60
  260.9 6.3 %all-to-all-done.9 = f32[16,2,512]{2,1,0:T(2,128)S(1)} async-done(((f32[16,2,512]{2,1,0:T(2,128)}), f32[16,2,512]{2,1,0:T(2,128)S(1)}, u32[]{:S(2)}, u32[]{:S(2)}) %all-to-all-start.9) | async-done | bytes 65568 | tf_op jit(solution)/shard_map/all_to_all | solution.py:63
  267.3 0.2 fusion.24
  267.5 0.7 fusion.26
  (27 shorter events, 0.7 us)
Async XLA Ops:
  25.9 12.5 %copy-start.1 = (bf16[512,512]{1,0:T(8,128)(2,1)S(1)}, bf16[512,512]{1,0:T(8,128)(2,1)}, u32[]{:S(2)}) copy-start(bf16[512,512]{1,0:T(8,128)(2,1)} %param.5) | copy-start | bytes 1572868
  25.9 61.6 %all-to-all-start.1 = ((bf16[16,32,2,2,512]{4,3,1,2,0:T(2,128)(2,1)}), bf16[16,32,2,2,512]{4,3,1,2,0:T(2,128)(2,1)}, u32[]{:S(2)}, u32[]{:S(2)}) async-start(bf16[16,32,2,2,512]{4,3,1,2,0:T(2,128)(2,1)} %broadcast_in_dim.17), calls=%async_computation.1 | async-start | bytes 4194304 | tf_op jit(solution)/shard_map/all_to_all | solution.py:21
  100.7 3.2 %copy-start = (f32[2,1024,512]{2,1,0:T(8,128)}, f32[2,1024,512]{2,1,0:T(8,128)S(1)}, u32[]{:S(2)}) copy-start(f32[2,1024,512]{2,1,0:T(8,128)S(1)} %fusion.19) | copy-start | bytes 12582916
  180.2 13.0 %all-to-all-start.7 = ((f32[32,1,1024]{2,1,0:T(1,128)}), f32[32,1,1024]{2,1,0:T(1,128)S(1)}, u32[]{:S(2)}, u32[]{:S(2)}) async-start(f32[32,1,1024]{2,1,0:T(1,128)} %broadcast_in_dim.44), calls=%async_computation.7 | async-start | bytes 262144 | tf_op jit(solution)/shard_map/all_to_all | solution.py:21
  197.7 54.2 %all-to-all-start.8 = ((f32[32,32,512]{2,1,0:T(8,128)}), f32[32,32,512]{2,1,0:T(8,128)}, u32[]{:S(2)}, u32[]{:S(2)}) async-start(f32[32,32,512]{2,1,0:T(8,128)} %fusion.16), calls=%async_computation.8 | async-start | bytes 4194304 | tf_op jit(solution)/shard_map/all_to_all | solution.py:63
  254.3 12.9 %all-to-all-start.9 = ((f32[16,2,512]{2,1,0:T(2,128)}), f32[16,2,512]{2,1,0:T(2,128)S(1)}, u32[]{:S(2)}, u32[]{:S(2)}) async-start(f32[16,2,512]{2,1,0:T(2,128)} %reshape.136), calls=%async_computation.9 | async-start | bytes 131072 | tf_op jit(solution)/shard_map/all_to_all | solution.py:63
  259.4 7.9 %copy-start.2 = (bf16[2,512]{1,0:T(2,128)(2,1)S(1)}, bf16[2,512]{1,0:T(2,128)(2,1)}, u32[]{:S(2)}) copy-start(bf16[2,512]{1,0:T(2,128)(2,1)} %param.3) | copy-start | bytes 6148
where the time goes:
time: 269 us; the launch traced here: 268 us
  waiting for transfers between devices  107 us (40%)
  blocking collectives  85.7 us (32%)
  starting transfers between devices  26.2 us (10%)
  local copies, waits for them, and re-layouts  20.2 us (8%)
  other arithmetic  16.9 us (6%)
  matrix products  11 us (4%)
    all_to_all x6, blocking collectives, from_everyone(): return lax.all_to_all(copies, axis, split_axis=0, concat_axis=0, tiled=True)  85.7 us
    all_to_all x2, waiting for transfers between devices, from_everyone(): return lax.all_to_all(copies, axis, split_axis=0, concat_axis=0, tiled=True)  57.7 us
    all_to_all x2, waiting for transfers between devices, sum_at_owner(): lax.all_to_all(parts, axis, split_axis=0, concat_axis=0, tiled=True)  49.5 us
    all_to_all x2, starting transfers between devices, from_everyone(): return lax.all_to_all(copies, axis, split_axis=0, concat_axis=0, tiled=True)  16.4 us
    all_to_all x2, starting transfers between devices, sum_at_owner(): lax.all_to_all(parts, axis, split_axis=0, concat_axis=0, tiled=True)  9.83 us
  transfers between devices with their start and end apart: 4, of which 4 were waited for; matrix products, arithmetic and copies ran while one was open for 3% of the time, Pallas kernels for 0%

commit v1 on v0

v1 whole, which is shorter than its diff:
```python
import functools

import jax
import jax.numpy as jnp
from jax import lax
from jax.experimental import pallas as pl
from jax.experimental.pallas import tpu as pltpu
from jax.sharding import Mesh
from jax.sharding import PartitionSpec as P

MESH = pl.DeviceIdType.MESH
AXES = ("wide_0", "wide_1", "narrow_0", "narrow_1")
SINK_ITERS = 3
NX, NU, CORES = 4, 8, 2
D = 512
OWN = 2
ROWS = NX * NU * NU * CORES * OWN
HALF = ROWS // CORES
SLAB = HALF // NX
TILE = NU * OWN
PROTOS = 512
BLOCK = 64
LANES = 128
TALL = ROWS // LANES
CUT = D // 2

epsilon = 1e-06
teacher_temp = 0.07
student_temp = 0.1

f32 = jnp.float32
bf16 = jnp.bfloat16


def inverse_norm(wide):
    return lax.rsqrt(jnp.sum(wide * wide, axis=1, keepdims=True) + epsilon)


def kernel(
    student_ref,
    teacher_ref,
    proto_ref,
    sgrad_ref,
    pgrad_ref,
    first,
    stage,
    gat_t,
    gat_s,
    proto_hat,
    proto_inv,
    e_t,
    e_s,
    cols,
    grad,
    near_src,
    near,
    far_src,
    far,
    part,
    other,
    cross,
    xbuf,
    ubuf,
    xslots,
    uslots,
    xsum,
    xuslots,
    xvsrc,
    xvslots,
    uvsrc,
    uvslots,
    first_send,
    first_recv,
    gat_send,
    gat_recv,
    swap_send,
    swap_recv,
    near_send,
    near_recv,
    far_send,
    far_recv,
    cross_send,
    cross_recv,
    big_send,
    big_recv,
    end_send,
    end_recv,
):
    x, y, z, c = (lax.axis_index(a) for a in AXES)
    u = z + c * (y - z)
    v = y + c * (z - y)
    oc = 1 - c

    def device(px, pu, pv):
        return (px, pv + c * (pu - pv), pu + c * (pv - pu), c)

    mate = (x, y, z, oc)

    def wait(ref, sem):
        pltpu.make_async_copy(ref, ref, sem).wait()

    def push(src, dst, send, recv, target):
        pltpu.make_async_remote_copy(
            src_ref=src, dst_ref=dst, send_sem=send, recv_sem=recv, device_id=target, device_id_type=MESH
        ).start()

    barrier = pltpu.get_barrier_semaphore()

    def greet_near(k, _):
        q = lax.rem(z * CORES + c + k, NU * CORES)
        pl.semaphore_signal(barrier, inc=1, device_id=(x, y, q // CORES, lax.rem(q, CORES)), device_id_type=MESH)
        return 0

    def greet_far(k, _):
        q = lax.rem(x * NU + y + k, NX * NU)
        pl.semaphore_signal(barrier, inc=1, device_id=(q // NU, lax.rem(q, NU), z, c), device_id_type=MESH)
        return 0

    def greet_side(k, _):
        px = lax.rem(x + 1 + k // (NU - 1), NX)
        pz = lax.rem(z + 1 + lax.rem(k, NU - 1), NU)
        pl.semaphore_signal(barrier, inc=1, device_id=(px, y, pz, c), device_id_type=MESH)
        return 0

    lax.fori_loop(1, NX * NU, greet_far, 0)
    lax.fori_loop(0, (NX - 1) * (NU - 1), greet_side, 0)
    lax.fori_loop(1, NU * CORES, greet_near, 0)

    wide_s = student_ref[...].astype(f32)
    wide_t = teacher_ref[...].astype(f32)
    s_inv = inverse_norm(wide_s)
    s_unit = wide_s * s_inv
    t_unit = wide_t * inverse_norm(wide_t)
    first[v, 0:OWN, :] = s_unit
    first[v, OWN : 2 * OWN, :] = t_unit

    def norm_block(i, _):
        at = pl.ds(pl.multiple_of(i * BLOCK, BLOCK), BLOCK)
        wide = proto_ref[at, :].astype(f32)
        inv = inverse_norm(wide)
        proto_inv[at, :] = jnp.broadcast_to(inv, (BLOCK, LANES))
        proto_hat[at, :] = (wide * inv).astype(bf16)
        return 0

    lax.fori_loop(0, PROTOS // BLOCK, norm_block, 0)

    pl.semaphore_wait(barrier, NU * CORES - 1 + NX * NU - 1 + (NX - 1) * (NU - 1))

    def send_first(k, _):
        push(first.at[v], first.at[v], first_send, first_recv, device(x, u, lax.rem(v + k, NU)))
        return 0

    lax.fori_loop(1, NU, send_first, 0)
    wait(first.at[pl.ds(0, NU - 1)], first_recv)
    for i in range(NU):
        stage[0, OWN * i : OWN * (i + 1), :] = first[i, 0:OWN, :]
        stage[1, OWN * i : OWN * (i + 1), :] = first[i, OWN : 2 * OWN, :]
    mine = pl.ds(pl.multiple_of(c * HALF + x * SLAB + u * TILE, TILE), TILE)
    gat_s[mine, :] = stage[0].astype(bf16)
    gat_t[mine, :] = stage[1].astype(bf16)

    def spread(buf, n):
        def send(k, _):
            q = lax.rem(x * NU + u + k, NX * NU)
            push(buf.at[mine], buf.at[mine], gat_send.at[n], gat_recv.at[n, x], device(q // NU, lax.rem(q, NU), v))
            return 0

        lax.fori_loop(1, NX * NU, send, 0)

    def slab(core, px):
        return pl.ds(pl.multiple_of(core * HALF + px * SLAB, SLAB), SLAB)

    def relay(buf, n):
        for k in range(NX):
            px = lax.rem(x + k, NX)
            wait(buf.at[pl.ds(0, SLAB - TILE if k == 0 else SLAB)], gat_recv.at[n, px])
            here = slab(c, px)
            push(buf.at[here], buf.at[here], swap_send.at[n], swap_recv.at[n], mate)

    def settle(buf, n):
        wait(buf.at[pl.ds(0, HALF)], swap_recv.at[n])
        wait(buf.at[pl.ds(0, HALF - TILE)], gat_send.at[n])
        wait(buf.at[pl.ds(0, HALF)], swap_send.at[n])

    spread(gat_t, 1)
    spread(gat_s, 0)
    wait(first.at[pl.ds(0, NU - 1)], first_send)
    relay(gat_t, 1)
    settle(gat_t, 1)

    def exponentials(buf, out, temp):
        for k in range(ROWS // 256):
            at = slice(k * 256, (k + 1) * 256)
            product = lax.dot_general(
                proto_hat[...], buf[at, :], (((1,), (1,)), ((), ())), preferred_element_type=f32
            )
            out[:, at] = jnp.exp(product * (1.0 / temp))

    def folded(value):
        return jnp.sum(value.reshape(BLOCK // 8, 8, ROWS), axis=0)

    def flat(ref):
        return jnp.concatenate([ref[k : k + 1, :] for k in range(TALL)], axis=1)

    def put(dst, at, acc):
        for k in range(TALL):
            dst[at + k : at + k + 1, :] = jnp.sum(acc[:, k * LANES : (k + 1) * LANES], axis=0, keepdims=True)

    def sweep(scale):
        def body(i, acc):
            at = pl.ds(pl.multiple_of(i * BLOCK, BLOCK), BLOCK)
            e = e_t[at, :]
            weighed = e if scale is None else e * scale
            col = 1.0 / jnp.sum(weighed, axis=1, keepdims=True)
            cols[at, :] = jnp.broadcast_to(col, (BLOCK, LANES))
            return acc + folded(e * col)

        return lax.fori_loop(0, PROTOS // BLOCK, body, jnp.zeros((8, ROWS), f32))

    def near_start(n, tall):
        me = z * CORES + c

        def send(k, _):
            q = lax.rem(me + k, NU * CORES)
            src = near_src.at[n, pl.ds(0, tall)]
            push(src, near.at[n, me, pl.ds(0, tall)], near_send.at[n], near_recv.at[n], (x, y, q // CORES, lax.rem(q, CORES)))
            return 0

        lax.fori_loop(1, NU * CORES, send, 0)
        near[n, me, 0:tall, :] = near_src[n, 0:tall, :]

    def near_end(n, tall):
        for sem in (near_recv, near_send):
            wait(near.at[n, pl.ds(0, NU * CORES - 1), pl.ds(0, tall)], sem.at[n])
        far_src[n, 0:tall, :] = jnp.sum(near[n, :, 0:tall, :], axis=0)

    def far_start(n, tall):
        me = x * NU + y

        def send(k, _):
            q = lax.rem(me + k, NX * NU)
            src = far_src.at[n, pl.ds(0, tall)]
            push(src, far.at[n, me, pl.ds(0, tall)], far_send.at[n], far_recv.at[n], (q // NU, lax.rem(q, NU), z, c))
            return 0

        lax.fori_loop(1, NX * NU, send, 0)
        far[n, me, 0:tall, :] = far_src[n, 0:tall, :]

    def far_end(n, tall):
        for sem in (far_recv, far_send):
            wait(far.at[n, pl.ds(0, NX * NU - 1), pl.ds(0, tall)], sem.at[n])
        return 1.0 / jnp.sum(far[n, :, 0:tall, :], axis=0)

    def row_of(inverse):
        part[...] = inverse
        return flat(part)

    exponentials(gat_t, e_t, teacher_temp)
    put(near_src.at[0], 0, sweep(None))
    near_start(0, TALL)
    relay(gat_s, 0)
    near_end(0, TALL)
    far_start(0, TALL)
    settle(gat_s, 0)
    exponentials(gat_s, e_s, student_temp)

    def student_sum(i, acc):
        at = pl.ds(pl.multiple_of(i * BLOCK, BLOCK), BLOCK)
        return acc + folded(e_s[at, :])

    put(near_src.at[1], TALL, lax.fori_loop(0, PROTOS // BLOCK, student_sum, jnp.zeros((8, ROWS), f32)))
    row_scale = row_of(far_end(0, TALL))
    put(near_src.at[1], 0, sweep(row_scale))
    near_start(1, 2 * TALL)
    near_end(1, 2 * TALL)
    far_start(1, 2 * TALL)
    both = far_end(1, 2 * TALL)
    row_scale = row_of(both[0:TALL])
    put(near_src.at[2], 0, sweep(row_scale))
    near_start(2, TALL)

    student_scale = row_of(both[TALL:] * (1.0 / student_temp))

    def scale_block(i, _):
        at = pl.ds(pl.multiple_of(i * BLOCK, BLOCK), BLOCK)
        e_s[at, :] = e_s[at, :] * student_scale
        e_t[at, :] = e_t[at, :] * cols[at, 0:1]
        return 0

    lax.fori_loop(0, PROTOS // BLOCK, scale_block, 0)
    near_end(2, TALL)
    far_start(2, TALL)
    row_scale = row_of(far_end(2, TALL) * (1.0 / student_temp))

    def grad_block(i, _):
        at = pl.ds(pl.multiple_of(i * BLOCK, BLOCK), BLOCK)
        grad[at, :] = (e_s[at, :] - e_t[at, :] * row_scale).astype(bf16)
        return 0

    lax.fori_loop(0, PROTOS // BLOCK, grad_block, 0)

    def row_product(core, k):
        at = pl.ds(pl.multiple_of(core * HALF + k * 256, 256), 256)
        return lax.dot_general(grad[:, at], proto_hat[...], (((0,), (0,)), ((), ())), preferred_element_type=f32)

    for k in range(HALF // 256):
        at = pl.ds(k * 256, 256)
        other[at, :] = row_product(oc, k)
        push(other.at[at], cross.at[at], cross_send, cross_recv.at[k], mate)
    per = 256 // SLAB
    for k in range(HALF // 256):
        at = pl.ds(k * 256, 256)
        mine_part = row_product(c, k)
        wait(cross.at[at], cross_recv.at[k])
        total = mine_part + cross[at, :]
        xbuf[pl.ds(k * per, per)] = total[:, :CUT].reshape(per, SLAB, CUT)
        ubuf[pl.ds(k * per, per)] = total[:, CUT:].reshape(per, NU, TILE, CUT)

    def send_x(k, _):
        px = lax.rem(x + k, NX)
        push(xbuf.at[px], xslots.at[x], big_send.at[0], big_recv.at[0], device(px, u, v))
        return 0

    def send_u(k, _):
        pu = lax.rem(u + k, NU)
        push(ubuf.at[:, pu], uslots.at[u], big_send.at[1], big_recv.at[1], device(x, pu, v))
        return 0

    lax.fori_loop(1, NX, send_x, 0)
    lax.fori_loop(1, NU, send_u, 0)
    xslots[x] = xbuf[x]
    uslots[u] = ubuf[:, u]

    def proto_block(i):
        at = slice(i * 256, (i + 1) * 256)
        step = jnp.dot(grad[at, :], gat_s[...], preferred_element_type=f32)
        inv = proto_inv[at, 0:1]
        unit = proto_ref[at, :].astype(f32) * inv
        pgrad_ref[at, :] = (step - unit * jnp.sum(unit * step, axis=1, keepdims=True)) * inv

    for i in range(PROTOS // 256):
        proto_block(i)

    for sem in (big_recv, big_send):
        wait(xslots.at[pl.ds(0, NX - 1)], sem.at[0])
    xsum[...] = jnp.sum(xslots[...], axis=0)

    def send_xu(k, _):
        pu = lax.rem(u + k, NU)
        src = xsum.at[pl.ds(pl.multiple_of(pu * TILE, TILE), TILE)]
        push(src, xuslots.at[u], end_send.at[0], end_recv.at[0], device(x, pu, v))
        return 0

    lax.fori_loop(1, NU, send_xu, 0)
    xuslots[u] = xsum[pl.ds(pl.multiple_of(u * TILE, TILE), TILE), :]

    for sem in (big_recv, big_send):
        wait(uslots.at[pl.ds(0, NU - 1)], sem.at[1])
    usum = jnp.sum(uslots[...], axis=0)
    for px in range(NX):
        for pv in range(NU):
            uvsrc[px * NU + pv] = usum[px, pv * OWN : (pv + 1) * OWN, :]

    def send_uv(k, _):
        q = lax.rem(x * NU + v + k, NX * NU)
        push(uvsrc.at[q], uvslots.at[x * NU + v], end_send.at[1], end_recv.at[1], device(q // NU, u, lax.rem(q, NU)))
        return 0

    lax.fori_loop(1, NX * NU, send_uv, 0)
    uvslots[x * NU + v] = uvsrc[x * NU + v]

    for sem in (end_recv, end_send):
        wait(xuslots.at[pl.ds(0, NU - 1)], sem.at[0])
    xusum = jnp.sum(xuslots[...], axis=0)
    for pv in range(NU):
        xvsrc[pv] = xusum[pv * OWN : (pv + 1) * OWN, :]

    def send_xv(k, _):
        pv = lax.rem(v + k, NU)
        push(xvsrc.at[pv], xvslots.at[v], end_send.at[2], end_recv.at[2], device(x, u, pv))
        return 0

    lax.fori_loop(1, NU, send_xv, 0)
    xvslots[v] = xvsrc[v]

    for sem in (end_recv, end_send):
        wait(uvslots.at[pl.ds(0, NX * NU - 1)], sem.at[1])
    right = jnp.sum(uvslots[...], axis=0)
    for sem in (end_recv, end_send):
        wait(xvslots.at[pl.ds(0, NU - 1)], sem.at[2])
    left = jnp.sum(xvslots[...], axis=0)
    wait(other, cross_send)

    step = jnp.concatenate([left, right], axis=1)
    sgrad_ref[...] = (step - s_unit * jnp.sum(s_unit * step, axis=1, keepdims=True)) * s_inv


def on_device(student, teacher, protos):
    vmem = pl.BlockSpec(memory_space=pltpu.VMEM)
    dma = pltpu.SemaphoreType.DMA
    return pl.pallas_call(
        kernel,
        out_shape=(
            jax.ShapeDtypeStruct((OWN, D), f32),
            jax.ShapeDtypeStruct((PROTOS, D), f32),
        ),
        in_specs=[vmem] * 3,
        out_specs=(vmem, vmem),
        scratch_shapes=[
            pltpu.VMEM((NU, 2 * OWN, D), f32),
            pltpu.VMEM((2, TILE, D), f32),
            pltpu.VMEM((ROWS, D), bf16),
            pltpu.VMEM((ROWS, D), bf16),
            pltpu.VMEM((PROTOS, D), bf16),
            pltpu.VMEM((PROTOS, LANES), f32),
            pltpu.VMEM((PROTOS, ROWS), f32),
            pltpu.VMEM((PROTOS, ROWS), f32),
            pltpu.VMEM((PROTOS, LANES), f32),
            pltpu.VMEM((PROTOS, ROWS), bf16),
            pltpu.VMEM((SINK_ITERS, 2 * TALL, LANES), f32),
            pltpu.VMEM((SINK_ITERS, NU * CORES, 2 * TALL, LANES), f32),
            pltpu.VMEM((SINK_ITERS, 2 * TALL, LANES), f32),
            pltpu.VMEM((SINK_ITERS, NX * NU, 2 * TALL, LANES), f32),
            pltpu.VMEM((TALL, LANES), f32),
            pltpu.VMEM((HALF, D), f32),
            pltpu.VMEM((HALF, D), f32),
            pltpu.VMEM((NX, SLAB, CUT), f32),
            pltpu.VMEM((NX, NU, TILE, D - CUT), f32),
            pltpu.VMEM((NX, SLAB, CUT), f32),
            pltpu.VMEM((NU, NX, TILE, D - CUT), f32),
            pltpu.VMEM((SLAB, CUT), f32),
            pltpu.VMEM((NU, TILE, CUT), f32),
            pltpu.VMEM((NU, OWN, CUT), f32),
            pltpu.VMEM((NU, OWN, CUT), f32),
            pltpu.VMEM((NX * NU, OWN, D - CUT), f32),
            pltpu.VMEM((NX * NU, OWN, D - CUT), f32),
            dma,
            dma,
            dma((2,)),
            dma((2, NX)),
            dma((2,)),
            dma((2,)),
            dma((SINK_ITERS,)),
            dma((SINK_ITERS,)),
            dma((SINK_ITERS,)),
            dma((SINK_ITERS,)),
            dma,
            dma((2,)),
            dma((2,)),
            dma((2,)),
            dma((3,)),
            dma((3,)),
        ],
        compiler_params=pltpu.CompilerParams(
            collective_id=0, has_side_effects=True, vmem_limit_bytes=48 << 20
        ),
        name="prototype_head",
    )(student, teacher, protos)


def solution(mesh):
    torus = Mesh(mesh.devices.reshape(NX, NU, NU, CORES), AXES)
    return jax.shard_map(
        on_device,
        mesh=torus,
        in_specs=(P(AXES, None),) * 3,
        out_specs=(P(AXES, None), P(AXES, None)),
        check_vma=False,
    )
```

time: 269 us -> 104 us (0.39)
  waiting for transfers between devices: 107 us -> 0 us
  Pallas kernels: 0 us -> 98.9 us
  blocking collectives: 85.7 us -> 0 us
  starting transfers between devices: 26.2 us -> 0 us
  other arithmetic: 16.9 us -> 0 us
  local copies, waits for them, and re-layouts: 20.2 us -> 3.96 us
  matrix products: 11 us -> 0 us
    all_to_all x4 -> x0, waiting for transfers between devices: 107 us -> none  [the longest x2 57.7 us: from_everyone(): return lax.all_to_all(copies, axis, split_axis=0, concat_axis=0, tiled=True)]
    pallas_call x0 -> x1, Pallas kernels: none -> 98.9 us  [on_device(): pl.pallas_call(kernel, out_shape=(jax.ShapeDtypeStruct((OWN, D), f32), ja...]
    all_to_all x6 -> x0, blocking collectives: 85.7 us -> none  [from_everyone(): return lax.all_to_all(copies, axis, split_axis=0, concat_axis=0, tiled=True)]
    all_to_all x4 -> x0, starting transfers between devices: 26.2 us -> none  [the longest x2 16.4 us: from_everyone(): return lax.all_to_all(copies, axis, split_axis=0, concat_axis=0, tiled=True)]
    reduce_sum x18 -> x0, other arithmetic: 15.2 us -> none  [the longest x2 4.02 us: on_device(): jnp.sum(exp_teacher * col_scale[None, :], axis=1)]
    dot_general x3 -> x0, matrix products: 11 us -> none  [the longest x1 4.34 us: on_device(): jnp.einsum('bp,pd->bd', grad_logits, proto_hat, preferred_element_type=jn...]
    reshape x2 -> x0, local copies, waits for them, and re-layouts: 4.78 us -> none  [the longest x1 4.12 us: in_order(): return jnp.moveaxis(parts, 0, dim).reshape(shape)]
    broadcast_in_dim x8 -> x0, local copies, waits for them, and re-layouts: 4.33 us -> none  [from_everyone(): copies = jnp.broadcast_to(shard, (lax.axis_size(axis), *shard.shape))]
  transfers between devices with their start and end apart: 4 -> 0, of which waited for: 4 -> 0; matrix products, arithmetic and copies ran while one was open for 3% -> 0% of each run, Pallas kernels for 0% -> 0%
where the time goes in v1:
time: 104 us; the launch traced here: 103 us
  Pallas kernels  98.9 us (95%)
  local copies, waits for them, and re-layouts  3.96 us (4%)
    pallas_call x1, Pallas kernels, on_device(): pl.pallas_call(kernel, out_shape=(jax.ShapeDtypeStruct((OWN, D), f32), ja...  98.9 us
    unnamed x8, local copies, waits for them, and re-layouts  3.96 us

profile of v1, /device:TPU:1, one launch (start us, length us, event | category | flops | bytes accessed | tf_op | source)
XLA Modules:
  0.0 103.5 jit_solution(15821042498093179617)
XLA Ops:
  0.6 0.0 copy-start
  0.6 1.0 copy-done
  1.7 0.0 copy-start.1
  1.7 0.7 copy-done.1
  2.4 0.0 copy-start.2
  2.4 0.7 copy-done.2
  3.0 98.9 %prototype_head.1 = (f32[2,512]{1,0:T(2,128)S(1)}, f32[512,512]{1,0:T(8,128)S(1)}) custom-call(bf16[2,512]{1,0:T(2,128)(2,1)S(1)} %copy-done.1, bf16[2,512]{1,0:T(2,128)(2,1)S(1)} %copy-done.2, bf16[512,512]{1,0:T(8,128)(2,1)S(1)} %copy-done), custom_call_target="tpu_custom_call" | custom-call | tf_op jit(solution)/shard_map/prototype_head/pallas_call | solution.py:401
  101.9 0.6 copy.7
  102.5 1.0 copy.8
Async XLA Ops:
  0.6 1.0 %copy-start = (bf16[512,512]{1,0:T(8,128)(2,1)S(1)}, bf16[512,512]{1,0:T(8,128)(2,1)}, u32[]{:S(2)}) copy-start(bf16[512,512]{1,0:T(8,128)(2,1)} %proto_ref.1) | copy-start | bytes 1572868
  1.7 0.7 copy-start.1
  2.4 0.7 copy-start.2

commit v2 on v1

v2 whole, which is shorter than its diff:
```python
import functools

import jax
import jax.numpy as jnp
from jax import lax
from jax.experimental import pallas as pl
from jax.experimental.pallas import tpu as pltpu
from jax.sharding import Mesh
from jax.sharding import PartitionSpec as P

MESH = pl.DeviceIdType.MESH
AXES = ("wide_0", "wide_1", "narrow_0", "narrow_1")
SUMS = 4
NX, NU, CORES = 4, 8, 2
D = 512
OWN = 2
ROWS = NX * NU * NU * CORES * OWN
HALF = ROWS // CORES
SLAB = HALF // NX
TILE = NU * OWN
PROTOS = 512
BLOCK = 64
LANES = 128
TALL = ROWS // LANES
CUT = D // 2

epsilon = 1e-06
teacher_temp = 0.07
student_temp = 0.1

f32 = jnp.float32
bf16 = jnp.bfloat16


def inverse_norm(wide):
    return lax.rsqrt(jnp.sum(wide * wide, axis=1, keepdims=True) + epsilon)


def kernel(
    student_hbm,
    teacher_hbm,
    proto_hbm,
    sgrad_ref,
    pgrad_ref,
    student_ref,
    teacher_ref,
    proto_ref,
    first,
    stage,
    gat_t,
    gat_s,
    proto_hat,
    proto_inv,
    e_t,
    e_s,
    cols,
    grad,
    near_src,
    near,
    far_src,
    far,
    part,
    other,
    cross,
    xbuf,
    ubuf,
    xslots,
    uslots,
    xsum,
    xuslots,
    xvsrc,
    xvslots,
    uvsrc,
    uvslots,
    load,
    first_send,
    first_recv,
    gat_send,
    gat_recv,
    swap_send,
    swap_recv,
    near_send,
    near_recv,
    far_send,
    far_recv,
    cross_send,
    cross_recv,
    big_send,
    big_recv,
    end_send,
    end_recv,
):
    x, y, z, c = (lax.axis_index(a) for a in AXES)
    u = z + c * (y - z)
    v = y + c * (z - y)
    oc = 1 - c

    def device(px, pu, pv):
        return (px, pv + c * (pu - pv), pu + c * (pv - pu), c)

    mate = (x, y, z, oc)

    def turned(at, k, n):
        return lax.rem(at + n // 2 + (1 - 2 * lax.rem(k, 2)) * ((k + 1) // 2), n)

    def near_peer(k):
        return (x, y, turned(z, k // CORES, NU), lax.rem(c + 1 + lax.rem(k, CORES), CORES))

    def far_peer(k):
        return (turned(x, lax.rem(k, NX), NX), turned(y, k // NX, NU), z, c)

    def plane(k, at):
        return turned(x, lax.rem(k, NX), NX), turned(at, k // NX, NU)

    def wait(ref, sem):
        pltpu.make_async_copy(ref, ref, sem).wait()

    def push(src, dst, send, recv, target):
        pltpu.make_async_remote_copy(
            src_ref=src, dst_ref=dst, send_sem=send, recv_sem=recv, device_id=target, device_id_type=MESH
        ).start()

    barrier = pltpu.get_barrier_semaphore()

    def greet(target):
        pl.semaphore_signal(barrier, inc=1, device_id=target, device_id_type=MESH)
        return 0

    def greet_side(k, _):
        return greet((turned(x, lax.rem(k, NX - 1), NX), y, turned(z, k // (NX - 1), NU), c))

    lax.fori_loop(0, NX * NU - 1, lambda k, _: greet(far_peer(k)), 0)
    lax.fori_loop(0, (NX - 1) * (NU - 1), greet_side, 0)
    lax.fori_loop(0, NU * CORES - 1, lambda k, _: greet(near_peer(k)), 0)

    inputs = [
        pltpu.make_async_copy(src, dst, load.at[i])
        for i, (src, dst) in enumerate(
            ((student_hbm, student_ref), (teacher_hbm, teacher_ref), (proto_hbm, proto_ref))
        )
    ]
    for copy in inputs:
        copy.start()
    for copy in inputs[:2]:
        copy.wait()

    wide_s = student_ref[...].astype(f32)
    wide_t = teacher_ref[...].astype(f32)
    s_inv = inverse_norm(wide_s)
    s_unit = wide_s * s_inv
    t_unit = wide_t * inverse_norm(wide_t)
    first[v, 0:OWN, :] = s_unit
    first[v, OWN : 2 * OWN, :] = t_unit

    def norm_block(i, _):
        at = pl.ds(pl.multiple_of(i * BLOCK, BLOCK), BLOCK)
        wide = proto_ref[at, :].astype(f32)
        inv = inverse_norm(wide)
        proto_inv[at, :] = jnp.broadcast_to(inv, (BLOCK, LANES))
        proto_hat[at, :] = (wide * inv).astype(bf16)
        return 0

    inputs[2].wait()
    lax.fori_loop(0, PROTOS // BLOCK, norm_block, 0)

    pl.semaphore_wait(barrier, NU * CORES - 1 + NX * NU - 1 + (NX - 1) * (NU - 1))

    def send_first(k, _):
        push(first.at[v], first.at[v], first_send, first_recv, device(x, u, turned(v, k, NU)))
        return 0

    lax.fori_loop(0, NU - 1, send_first, 0)
    wait(first.at[pl.ds(0, NU - 1)], first_recv)
    for i in range(NU):
        stage[0, OWN * i : OWN * (i + 1), :] = first[i, 0:OWN, :]
        stage[1, OWN * i : OWN * (i + 1), :] = first[i, OWN : 2 * OWN, :]
    mine = pl.ds(pl.multiple_of(c * HALF + x * SLAB + u * TILE, TILE), TILE)
    gat_s[mine, :] = stage[0].astype(bf16)
    gat_t[mine, :] = stage[1].astype(bf16)

    def spread(buf, n):
        def send(k, _):
            px, pu = plane(k, u)
            push(buf.at[mine], buf.at[mine], gat_send.at[n], gat_recv.at[n, x], device(px, pu, v))
            return 0

        lax.fori_loop(0, NX * NU - 1, send, 0)

    def slab(core, px):
        return pl.ds(pl.multiple_of(core * HALF + px * SLAB, SLAB), SLAB)

    def relay(buf, n):
        for k in range(NX):
            px = lax.rem(x + k, NX)
            wait(buf.at[pl.ds(0, SLAB - TILE if k == 0 else SLAB)], gat_recv.at[n, px])
            here = slab(c, px)
            push(buf.at[here], buf.at[here], swap_send.at[n], swap_recv.at[n], mate)

    def settle(buf, n):
        wait(buf.at[pl.ds(0, HALF)], swap_recv.at[n])
        wait(buf.at[pl.ds(0, HALF - TILE)], gat_send.at[n])
        wait(buf.at[pl.ds(0, HALF)], swap_send.at[n])

    spread(gat_t, 1)
    wait(first.at[pl.ds(0, NU - 1)], first_send)
    relay(gat_t, 1)
    settle(gat_t, 1)

    def exponentials(buf, out, temp):
        for k in range(ROWS // 256):
            at = slice(k * 256, (k + 1) * 256)
            product = lax.dot_general(
                proto_hat[...], buf[at, :], (((1,), (1,)), ((), ())), preferred_element_type=f32
            )
            out[:, at] = jnp.exp(product * (1.0 / temp))

    def folded(value):
        return jnp.sum(value.reshape(BLOCK // 8, 8, ROWS), axis=0)

    def flat(ref):
        return jnp.concatenate([ref[k : k + 1, :] for k in range(TALL)], axis=1)

    def put(dst, acc):
        for k in range(TALL):
            dst[k : k + 1, :] = jnp.sum(acc[:, k * LANES : (k + 1) * LANES], axis=0, keepdims=True)

    def sweep(scale):
        def body(i, acc):
            at = pl.ds(pl.multiple_of(i * BLOCK, BLOCK), BLOCK)
            e = e_t[at, :]
            weighed = e if scale is None else e * scale
            col = 1.0 / jnp.sum(weighed, axis=1, keepdims=True)
            cols[at, :] = jnp.broadcast_to(col, (BLOCK, LANES))
            return acc + folded(e * col)

        return lax.fori_loop(0, PROTOS // BLOCK, body, jnp.zeros((8, ROWS), f32))

    def near_start(n):
        me = z * CORES + c

        def send(k, _):
            push(near_src.at[n], near.at[n, me], near_send.at[n], near_recv.at[n], near_peer(k))
            return 0

        lax.fori_loop(0, NU * CORES - 1, send, 0)
        near[n, me] = near_src[n]

    def near_end(n):
        for sem in (near_recv, near_send):
            wait(near.at[n, pl.ds(0, NU * CORES - 1)], sem.at[n])
        far_src[n] = jnp.sum(near[n], axis=0)

    def far_start(n):
        me = x * NU + y

        def send(k, _):
            push(far_src.at[n], far.at[n, me], far_send.at[n], far_recv.at[n], far_peer(k))
            return 0

        lax.fori_loop(0, NX * NU - 1, send, 0)
        far[n, me] = far_src[n]

    def far_end(n):
        for sem in (far_recv, far_send):
            wait(far.at[n, pl.ds(0, NX * NU - 1)], sem.at[n])
        return 1.0 / jnp.sum(far[n], axis=0)

    def row_of(inverse):
        part[...] = inverse
        return flat(part)

    def student_sum(i, acc):
        at = pl.ds(pl.multiple_of(i * BLOCK, BLOCK), BLOCK)
        return acc + folded(e_s[at, :])

    exponentials(gat_t, e_t, teacher_temp)
    put(near_src.at[0], sweep(None))
    near_start(0)
    spread(gat_s, 0)
    near_end(0)
    far_start(0)
    relay(gat_s, 0)
    row_scale = row_of(far_end(0))

    put(near_src.at[1], sweep(row_scale))
    near_start(1)
    settle(gat_s, 0)
    exponentials(gat_s, e_s, student_temp)
    put(near_src.at[3], lax.fori_loop(0, PROTOS // BLOCK, student_sum, jnp.zeros((8, ROWS), f32)))
    near_start(3)
    near_end(1)
    far_start(1)
    near_end(3)
    far_start(3)
    row_scale = row_of(far_end(1))

    put(near_src.at[2], sweep(row_scale))
    near_start(2)
    student_scale = row_of(far_end(3) * (1.0 / student_temp))

    def scale_block(i, _):
        at = pl.ds(pl.multiple_of(i * BLOCK, BLOCK), BLOCK)
        e_s[at, :] = e_s[at, :] * student_scale
        e_t[at, :] = e_t[at, :] * cols[at, 0:1]
        return 0

    lax.fori_loop(0, PROTOS // BLOCK, scale_block, 0)
    near_end(2)
    far_start(2)
    row_scale = row_of(far_end(2) * (1.0 / student_temp))

    def grad_block(i, _):
        at = pl.ds(pl.multiple_of(i * BLOCK, BLOCK), BLOCK)
        grad[at, :] = (e_s[at, :] - e_t[at, :] * row_scale).astype(bf16)
        return 0

    lax.fori_loop(0, PROTOS // BLOCK, grad_block, 0)

    def row_product(at):
        return lax.dot_general(grad[:, at], proto_hat[...], (((0,), (0,)), ((), ())), preferred_element_type=f32)

    for k in range(NX):
        px = turned(x, k, NX)
        other[px] = row_product(slab(oc, px))
        push(other.at[px], cross.at[px], cross_send, cross_recv.at[px], mate)
    for k in range(NX):
        px = turned(x, k, NX)
        mine_part = row_product(slab(c, px))
        wait(cross.at[px], cross_recv.at[px])
        total = mine_part + cross[px]
        xbuf[px] = total[:, :CUT]
        ubuf[px] = total[:, CUT:].reshape(NU, TILE, D - CUT)
        if k < NX - 1:
            push(xbuf.at[px], xslots.at[x], big_send.at[0], big_recv.at[0], device(px, u, v))

    def send_u(k, _):
        pu = turned(u, k, NU)
        push(ubuf.at[:, pu], uslots.at[u], big_send.at[1], big_recv.at[1], device(x, pu, v))
        return 0

    lax.fori_loop(0, NU - 1, send_u, 0)
    xslots[x] = xbuf[x]
    uslots[u] = ubuf[:, u]

    def proto_block(i):
        at = slice(i * 256, (i + 1) * 256)
        step = jnp.dot(grad[at, :], gat_s[...], preferred_element_type=f32)
        inv = proto_inv[at, 0:1]
        unit = proto_ref[at, :].astype(f32) * inv
        pgrad_ref[at, :] = (step - unit * jnp.sum(unit * step, axis=1, keepdims=True)) * inv

    for i in range(PROTOS // 256):
        proto_block(i)

    for sem in (big_recv, big_send):
        wait(xslots.at[pl.ds(0, NX - 1)], sem.at[0])
    xsum[...] = jnp.sum(xslots[...], axis=0)

    def send_xu(k, _):
        pu = turned(u, k, NU)
        src = xsum.at[pl.ds(pl.multiple_of(pu * TILE, TILE), TILE)]
        push(src, xuslots.at[u], end_send.at[0], end_recv.at[0], device(x, pu, v))
        return 0

    lax.fori_loop(0, NU - 1, send_xu, 0)
    xuslots[u] = xsum[pl.ds(pl.multiple_of(u * TILE, TILE), TILE), :]

    for sem in (big_recv, big_send):
        wait(uslots.at[pl.ds(0, NU - 1)], sem.at[1])
    usum = jnp.sum(uslots[...], axis=0)
    for px in range(NX):
        for pv in range(NU):
            uvsrc[px * NU + pv] = usum[px, pv * OWN : (pv + 1) * OWN, :]

    def send_uv(k, _):
        px, pv = plane(k, v)
        push(uvsrc.at[px * NU + pv], uvslots.at[x * NU + v], end_send.at[1], end_recv.at[1], device(px, u, pv))
        return 0

    lax.fori_loop(0, NX * NU - 1, send_uv, 0)
    uvslots[x * NU + v] = uvsrc[x * NU + v]

    for sem in (end_recv, end_send):
        wait(xuslots.at[pl.ds(0, NU - 1)], sem.at[0])
    xusum = jnp.sum(xuslots[...], axis=0)
    for pv in range(NU):
        xvsrc[pv] = xusum[pv * OWN : (pv + 1) * OWN, :]

    def send_xv(k, _):
        pv = turned(v, k, NU)
        push(xvsrc.at[pv], xvslots.at[v], end_send.at[2], end_recv.at[2], device(x, u, pv))
        return 0

    lax.fori_loop(0, NU - 1, send_xv, 0)
    xvslots[v] = xvsrc[v]

    for sem in (end_recv, end_send):
        wait(uvslots.at[pl.ds(0, NX * NU - 1)], sem.at[1])
    right = jnp.sum(uvslots[...], axis=0)
    for sem in (end_recv, end_send):
        wait(xvslots.at[pl.ds(0, NU - 1)], sem.at[2])
    left = jnp.sum(xvslots[...], axis=0)
    wait(other, cross_send)

    step = jnp.concatenate([left, right], axis=1)
    sgrad_ref[...] = (step - s_unit * jnp.sum(s_unit * step, axis=1, keepdims=True)) * s_inv


def on_device(student, teacher, protos):
    vmem = pl.BlockSpec(memory_space=pltpu.VMEM)
    dma = pltpu.SemaphoreType.DMA
    return pl.pallas_call(
        kernel,
        out_shape=(
            jax.ShapeDtypeStruct((OWN, D), f32),
            jax.ShapeDtypeStruct((PROTOS, D), f32),
        ),
        in_specs=[pl.BlockSpec(memory_space=pltpu.HBM)] * 3,
        out_specs=(vmem, vmem),
        scratch_shapes=[
            pltpu.VMEM((OWN, D), bf16),
            pltpu.VMEM((OWN, D), bf16),
            pltpu.VMEM((PROTOS, D), bf16),
            pltpu.VMEM((NU, 2 * OWN, D), f32),
            pltpu.VMEM((2, TILE, D), f32),
            pltpu.VMEM((ROWS, D), bf16),
            pltpu.VMEM((ROWS, D), bf16),
            pltpu.VMEM((PROTOS, D), bf16),
            pltpu.VMEM((PROTOS, LANES), f32),
            pltpu.VMEM((PROTOS, ROWS), f32),
            pltpu.VMEM((PROTOS, ROWS), f32),
            pltpu.VMEM((PROTOS, LANES), f32),
            pltpu.VMEM((PROTOS, ROWS), bf16),
            pltpu.VMEM((SUMS, TALL, LANES), f32),
            pltpu.VMEM((SUMS, NU * CORES, TALL, LANES), f32),
            pltpu.VMEM((SUMS, TALL, LANES), f32),
            pltpu.VMEM((SUMS, NX * NU, TALL, LANES), f32),
            pltpu.VMEM((TALL, LANES), f32),
            pltpu.VMEM((NX, SLAB, D), f32),
            pltpu.VMEM((NX, SLAB, D), f32),
            pltpu.VMEM((NX, SLAB, CUT), f32),
            pltpu.VMEM((NX, NU, TILE, D - CUT), f32),
            pltpu.VMEM((NX, SLAB, CUT), f32),
            pltpu.VMEM((NU, NX, TILE, D - CUT), f32),
            pltpu.VMEM((SLAB, CUT), f32),
            pltpu.VMEM((NU, TILE, CUT), f32),
            pltpu.VMEM((NU, OWN, CUT), f32),
            pltpu.VMEM((NU, OWN, CUT), f32),
            pltpu.VMEM((NX * NU, OWN, D - CUT), f32),
            pltpu.VMEM((NX * NU, OWN, D - CUT), f32),
            dma((3,)),
            dma,
            dma,
            dma((2,)),
            dma((2, NX)),
            dma((2,)),
            dma((2,)),
            dma((SUMS,)),
            dma((SUMS,)),
            dma((SUMS,)),
            dma((SUMS,)),
            dma,
            dma((NX,)),
            dma((2,)),
            dma((2,)),
            dma((3,)),
            dma((3,)),
        ],
        compiler_params=pltpu.CompilerParams(
            collective_id=0, has_side_effects=True, vmem_limit_bytes=48 << 20
        ),
        name="prototype_head",
    )(*(pltpu.with_memory_space_constraint(a, pltpu.HBM) for a in (student, teacher, protos)))


def solution(mesh):
    torus = Mesh(mesh.devices.reshape(NX, NU, NU, CORES), AXES)
    return jax.shard_map(
        on_device,
        mesh=torus,
        in_specs=(P(AXES, None),) * 3,
        out_specs=(P(AXES, None), P(AXES, None)),
        check_vma=False,
    )
```

time: 104 us -> 95 us (0.913)
  Pallas kernels: 98.9 us -> 92.2 us
  local copies, waits for them, and re-layouts: 3.96 us -> 1.56 us
    pallas_call x1, Pallas kernels: 98.9 us -> 92.2 us  [on_device(): pl.pallas_call(kernel, out_shape=(jax.ShapeDtypeStruct((OWN, D), f32), ja...]
    unnamed x8 -> x2, local copies, waits for them, and re-layouts: 3.96 us -> 1.56 us
where the time goes in v2:
time: 95 us; the launch traced here: 94.4 us
  Pallas kernels  92.2 us (97%)
  local copies, waits for them, and re-layouts  1.56 us (2%)
    pallas_call x1, Pallas kernels, on_device(): pl.pallas_call(kernel, out_shape=(jax.ShapeDtypeStruct((OWN, D), f32), ja...  92.2 us

profile of v2, /device:TPU:1, one launch (start us, length us, event | category | flops | bytes accessed | tf_op | source)
XLA Modules:
  0.0 94.4 jit_solution(1198753486406820040)
XLA Ops:
  0.6 92.2 %prototype_head.1 = (f32[2,512]{1,0:T(2,128)S(1)}, f32[512,512]{1,0:T(8,128)S(1)}) custom-call(bf16[2,512]{1,0:T(2,128)(2,1)} %student_hbm.1, bf16[2,512]{1,0:T(2,128)(2,1)} %teacher_hbm.1, bf16[512,512]{1,0:T(8,128)(2,1)} %proto_hbm.1), custom_call_target="tpu_custom_call" | custom-call | tf_op jit(solution)/shard_map/prototype_head/pallas_call | solution.py:412
  92.8 0.6 copy.7
  93.4 1.0 %copy.8 = f32[512,512]{1,0:T(8,128)} copy(f32[512,512]{1,0:T(8,128)S(1)} %get-tuple-element.5) | data formatting | bytes 2097152

commit v3 on v2

--- a/solution.py
+++ b/solution.py
@@ -60,8 +60,9 @@
     far_src,
     far,
     part,
-    other,
-    cross,
+    own,
+    proto_mate,
+    grad_mate,
     xbuf,
     ubuf,
     xslots,
@@ -83,8 +84,8 @@
     near_recv,
     far_send,
     far_recv,
-    cross_send,
-    cross_recv,
+    mate_send,
+    mate_recv,
     big_send,
     big_recv,
     end_send,
@@ -178,21 +179,21 @@
     gat_s[mine, :] = stage[0].astype(bf16)
     gat_t[mine, :] = stage[1].astype(bf16)
 
-    def spread(buf, n):
+    def spread(buf, n, start=0, stop=NX * NU - 1):
         def send(k, _):
-            px, pu = plane(k, u)
+            px, pu = turned(x, k // NU, NX), turned(u, lax.rem(k, NU), NU)
             push(buf.at[mine], buf.at[mine], gat_send.at[n], gat_recv.at[n, x], device(px, pu, v))
             return 0
 
-        lax.fori_loop(0, NX * NU - 1, send, 0)
+        lax.fori_loop(start, stop, send, 0)
 
     def slab(core, px):
         return pl.ds(pl.multiple_of(core * HALF + px * SLAB, SLAB), SLAB)
 
     def relay(buf, n):
         for k in range(NX):
-            px = lax.rem(x + k, NX)
-            wait(buf.at[pl.ds(0, SLAB - TILE if k == 0 else SLAB)], gat_recv.at[n, px])
+            px = turned(x, k, NX)
+            wait(buf.at[pl.ds(0, SLAB - TILE if k == NX - 1 else SLAB)], gat_recv.at[n, px])
             here = slab(c, px)
             push(buf.at[here], buf.at[here], swap_send.at[n], swap_recv.at[n], mate)
 
@@ -202,6 +203,7 @@
         wait(buf.at[pl.ds(0, HALF)], swap_send.at[n])
 
     spread(gat_t, 1)
+    push(proto_hat, proto_mate, mate_send.at[0], mate_recv.at[0], mate)
     wait(first.at[pl.ds(0, NU - 1)], first_send)
     relay(gat_t, 1)
     settle(gat_t, 1)
@@ -276,26 +278,29 @@
     exponentials(gat_t, e_t, teacher_temp)
     put(near_src.at[0], sweep(None))
     near_start(0)
-    spread(gat_s, 0)
+    spread(gat_s, 0, 0, NX * NU // 2)
     near_end(0)
     far_start(0)
-    relay(gat_s, 0)
+    spread(gat_s, 0, NX * NU // 2)
     row_scale = row_of(far_end(0))
 
     put(near_src.at[1], sweep(row_scale))
     near_start(1)
+    relay(gat_s, 0)
+    near_end(1)
+    far_start(1)
     settle(gat_s, 0)
     exponentials(gat_s, e_s, student_temp)
     put(near_src.at[3], lax.fori_loop(0, PROTOS // BLOCK, student_sum, jnp.zeros((8, ROWS), f32)))
     near_start(3)
-    near_end(1)
-    far_start(1)
+    row_scale = row_of(far_end(1))
+
+    put(near_src.at[2], sweep(row_scale))
+    near_start(2)
     near_end(3)
     far_start(3)
-    row_scale = row_of(far_end(1))
-
-    put(near_src.at[2], sweep(row_scale))
-    near_start(2)
+    near_end(2)
+    far_start(2)
     student_scale = row_of(far_end(3) * (1.0 / student_temp))
 
     def scale_block(i, _):
@@ -305,29 +310,35 @@
         return 0
 
     lax.fori_loop(0, PROTOS // BLOCK, scale_block, 0)
-    near_end(2)
-    far_start(2)
-    row_scale = row_of(far_end(2) * (1.0 / student_temp))
-
-    def grad_block(i, _):
-        at = pl.ds(pl.multiple_of(i * BLOCK, BLOCK), BLOCK)
-        grad[at, :] = (e_s[at, :] - e_t[at, :] * row_scale).astype(bf16)
-        return 0
-
-    lax.fori_loop(0, PROTOS // BLOCK, grad_block, 0)
-
-    def row_product(at):
-        return lax.dot_general(grad[:, at], proto_hat[...], (((0,), (0,)), ((), ())), preferred_element_type=f32)
-
+    part[...] = far_end(2) * (1.0 / student_temp)
+
+    def gradients(core):
+        rows = [part[pl.ds(core * (TALL // CORES) + k, 1), :] for k in range(TALL // CORES)]
+        scale = jnp.concatenate(rows, axis=1)
+        lanes = pl.ds(pl.multiple_of(core * HALF, HALF), HALF)
+
+        def body(i, _):
+            at = pl.ds(pl.multiple_of(i * BLOCK, BLOCK), BLOCK)
+            grad[core, at, :] = (e_s[at, lanes] - e_t[at, lanes] * scale).astype(bf16)
+            return 0
+
+        lax.fori_loop(0, PROTOS // BLOCK, body, 0)
+
+    gradients(oc)
+    push(grad.at[oc], grad_mate, mate_send.at[1], mate_recv.at[1], mate)
+    gradients(c)
+
+    def row_product(left, px, right):
+        at = pl.ds(pl.multiple_of(px * SLAB, SLAB), SLAB)
+        return lax.dot_general(left[:, at], right[...], (((0,), (0,)), ((), ())), preferred_element_type=f32)
+
+    for px in range(NX):
+        own[px] = row_product(grad.at[c], px, proto_hat)
+    wait(proto_mate, mate_recv.at[0])
+    wait(grad_mate, mate_recv.at[1])
     for k in range(NX):
         px = turned(x, k, NX)
-        other[px] = row_product(slab(oc, px))
-        push(other.at[px], cross.at[px], cross_send, cross_recv.at[px], mate)
-    for k in range(NX):
-        px = turned(x, k, NX)
-        mine_part = row_product(slab(c, px))
-        wait(cross.at[px], cross_recv.at[px])
-        total = mine_part + cross[px]
+        total = own[px] + row_product(grad_mate, px, proto_mate)
         xbuf[px] = total[:, :CUT]
         ubuf[px] = total[:, CUT:].reshape(NU, TILE, D - CUT)
         if k < NX - 1:
@@ -344,7 +355,8 @@
 
     def proto_block(i):
         at = slice(i * 256, (i + 1) * 256)
-        step = jnp.dot(grad[at, :], gat_s[...], preferred_element_type=f32)
+        step = jnp.dot(grad[0, at, :], gat_s[:HALF, :], preferred_element_type=f32)
+        step += jnp.dot(grad[1, at, :], gat_s[HALF:, :], preferred_element_type=f32)
         inv = proto_inv[at, 0:1]
         unit = proto_ref[at, :].astype(f32) * inv
         pgrad_ref[at, :] = (step - unit * jnp.sum(unit * step, axis=1, keepdims=True)) * inv
@@ -400,7 +412,8 @@
     for sem in (end_recv, end_send):
         wait(xvslots.at[pl.ds(0, NU - 1)], sem.at[2])
     left = jnp.sum(xvslots[...], axis=0)
-    wait(other, cross_send)
+    wait(proto_mate, mate_send.at[0])
+    wait(grad_mate, mate_send.at[1])
 
     step = jnp.concatenate([left, right], axis=1)
     sgrad_ref[...] = (step - s_unit * jnp.sum(s_unit * step, axis=1, keepdims=True)) * s_inv
@@ -430,14 +443,15 @@
             pltpu.VMEM((PROTOS, ROWS), f32),
             pltpu.VMEM((PROTOS, ROWS), f32),
             pltpu.VMEM((PROTOS, LANES), f32),
-            pltpu.VMEM((PROTOS, ROWS), bf16),
+            pltpu.VMEM((CORES, PROTOS, HALF), bf16),
             pltpu.VMEM((SUMS, TALL, LANES), f32),
             pltpu.VMEM((SUMS, NU * CORES, TALL, LANES), f32),
             pltpu.VMEM((SUMS, TALL, LANES), f32),
             pltpu.VMEM((SUMS, NX * NU, TALL, LANES), f32),
             pltpu.VMEM((TALL, LANES), f32),
             pltpu.VMEM((NX, SLAB, D), f32),
-            pltpu.VMEM((NX, SLAB, D), f32),
+            pltpu.VMEM((PROTOS, D), bf16),
+            pltpu.VMEM((PROTOS, HALF), bf16),
             pltpu.VMEM((NX, SLAB, CUT), f32),
             pltpu.VMEM((NX, NU, TILE, D - CUT), f32),
             pltpu.VMEM((NX, SLAB, CUT), f32),
@@ -459,8 +473,8 @@
             dma((SUMS,)),
             dma((SUMS,)),
             dma((SUMS,)),
-            dma,
-            dma((NX,)),
+            dma((2,)),
+            dma((2,)),
             dma((2,)),
             dma((2,)),
             dma((3,)),

time: 95 us -> 92.4 us (0.973)
  Pallas kernels: 92.2 us -> 89.9 us
    pallas_call x1, Pallas kernels: 92.2 us -> 89.9 us  [on_device(): pl.pallas_call(kernel, out_shape=(jax.ShapeDtypeStruct((OWN, D), f32), ja...]
where the time goes in v3:
time: 92.4 us; the launch traced here: 92.1 us
  Pallas kernels  89.9 us (97%)
  local copies, waits for them, and re-layouts  1.56 us (2%)
    pallas_call x1, Pallas kernels, on_device(): pl.pallas_call(kernel, out_shape=(jax.ShapeDtypeStruct((OWN, D), f32), ja...  89.9 us

profile of v3, /device:TPU:1, one launch (start us, length us, event | category | flops | bytes accessed | tf_op | source)
XLA Modules:
  0.0 92.1 jit_solution(9889527650012912954)
XLA Ops:
  0.6 89.9 %prototype_head.1 = (f32[2,512]{1,0:T(2,128)S(1)}, f32[512,512]{1,0:T(8,128)S(1)}) custom-call(bf16[2,512]{1,0:T(2,128)(2,1)} %student_hbm.1, bf16[2,512]{1,0:T(2,128)(2,1)} %teacher_hbm.1, bf16[512,512]{1,0:T(8,128)(2,1)} %proto_hbm.1), custom_call_target="tpu_custom_call" | custom-call | tf_op jit(solution)/shard_map/prototype_head/pallas_call | solution.py:425
  90.5 0.6 copy.7
  91.1 1.0 %copy.8 = f32[512,512]{1,0:T(8,128)} copy(f32[512,512]{1,0:T(8,128)S(1)} %get-tuple-element.5) | data formatting | bytes 2097152

commit v4 on v3

--- a/solution.py
+++ b/solution.py
@@ -121,19 +121,6 @@
             src_ref=src, dst_ref=dst, send_sem=send, recv_sem=recv, device_id=target, device_id_type=MESH
         ).start()
 
-    barrier = pltpu.get_barrier_semaphore()
-
-    def greet(target):
-        pl.semaphore_signal(barrier, inc=1, device_id=target, device_id_type=MESH)
-        return 0
-
-    def greet_side(k, _):
-        return greet((turned(x, lax.rem(k, NX - 1), NX), y, turned(z, k // (NX - 1), NU), c))
-
-    lax.fori_loop(0, NX * NU - 1, lambda k, _: greet(far_peer(k)), 0)
-    lax.fori_loop(0, (NX - 1) * (NU - 1), greet_side, 0)
-    lax.fori_loop(0, NU * CORES - 1, lambda k, _: greet(near_peer(k)), 0)
-
     inputs = [
         pltpu.make_async_copy(src, dst, load.at[i])
         for i, (src, dst) in enumerate(
@@ -142,9 +129,22 @@
     ]
     for copy in inputs:
         copy.start()
+
+    barrier = pltpu.get_barrier_semaphore()
+
+    def greet(target):
+        pl.semaphore_signal(barrier, inc=1, device_id=target, device_id_type=MESH)
+        return 0
+
+    def greet_side(k, _):
+        return greet((turned(x, lax.rem(k, NX - 1), NX), y, turned(z, k // (NX - 1), NU), c))
+
+    lax.fori_loop(0, NX * NU - 1, lambda k, _: greet(far_peer(k)), 0)
+    lax.fori_loop(0, (NX - 1) * (NU - 1), greet_side, 0)
+    lax.fori_loop(0, NU * CORES - 1, lambda k, _: greet(near_peer(k)), 0)
+
     for copy in inputs[:2]:
         copy.wait()
-
     wide_s = student_ref[...].astype(f32)
     wide_t = teacher_ref[...].astype(f32)
     s_inv = inverse_norm(wide_s)
@@ -161,58 +161,90 @@
         proto_hat[at, :] = (wide * inv).astype(bf16)
         return 0
 
+    pl.semaphore_wait(barrier, NU * CORES - 1 + NX * NU - 1 + (NX - 1) * (NU - 1))
+
+    def send_first(k, _):
+        push(first.at[v], first.at[v], first_send, first_recv, device(x, u, turned(v, k, NU)))
+        return 0
+
+    lax.fori_loop(0, NU - 1, send_first, 0)
     inputs[2].wait()
     lax.fori_loop(0, PROTOS // BLOCK, norm_block, 0)
-
-    pl.semaphore_wait(barrier, NU * CORES - 1 + NX * NU - 1 + (NX - 1) * (NU - 1))
-
-    def send_first(k, _):
-        push(first.at[v], first.at[v], first_send, first_recv, device(x, u, turned(v, k, NU)))
-        return 0
-
-    lax.fori_loop(0, NU - 1, send_first, 0)
     wait(first.at[pl.ds(0, NU - 1)], first_recv)
     for i in range(NU):
         stage[0, OWN * i : OWN * (i + 1), :] = first[i, 0:OWN, :]
         stage[1, OWN * i : OWN * (i + 1), :] = first[i, OWN : 2 * OWN, :]
-    mine = pl.ds(pl.multiple_of(c * HALF + x * SLAB + u * TILE, TILE), TILE)
-    gat_s[mine, :] = stage[0].astype(bf16)
-    gat_t[mine, :] = stage[1].astype(bf16)
-
-    def spread(buf, n, start=0, stop=NX * NU - 1):
-        def send(k, _):
-            px, pu = turned(x, k // NU, NX), turned(u, lax.rem(k, NU), NU)
-            push(buf.at[mine], buf.at[mine], gat_send.at[n], gat_recv.at[n, x], device(px, pu, v))
-            return 0
-
-        lax.fori_loop(start, stop, send, 0)
-
-    def slab(core, px):
-        return pl.ds(pl.multiple_of(core * HALF + px * SLAB, SLAB), SLAB)
+    for h in range(2):
+        at = slice(h * CUT, (h + 1) * CUT)
+        gat_s[h, c, x, u] = stage[0, :, at].astype(bf16)
+        gat_t[h, c, x, u] = stage[1, :, at].astype(bf16)
+
+    def open_step(buf, n):
+        def send_hi(k, _):
+            block = buf.at[1, c, x, u]
+            push(block, block, gat_send.at[n, 1], gat_recv.at[n, 1], device(turned(x, k, NX), u, v))
+            return 0
+
+        def send_lo(k, _):
+            block = buf.at[0, c, x, u]
+            push(block, block, gat_send.at[n, 0], gat_recv.at[n, 0], device(x, turned(u, k, NU), v))
+            return 0
+
+        lax.fori_loop(0, NU - 1, send_lo, 0)
+        lax.fori_loop(0, NX - 1, send_hi, 0)
+
+    def spread_step(buf, n):
+        def send_hi(k, _):
+            block = buf.at[1, c, :, u]
+            push(block, block, gat_send.at[n, 2], gat_recv.at[n, 2], device(x, turned(u, k, NU), v))
+            return 0
+
+        def send_lo(k, _):
+            block = buf.at[0, c, x]
+            push(block, block, gat_send.at[n, 3], gat_recv.at[n, 3 + x], device(turned(x, k, NX), u, v))
+            return 0
+
+        wait(buf.at[0, 0, 0, pl.ds(0, NX - 1)], gat_recv.at[n, 1])
+        lax.fori_loop(0, NU - 1, send_hi, 0)
+        wait(buf.at[0, 0, 0, pl.ds(0, NU - 1)], gat_recv.at[n, 0])
+        lax.fori_loop(0, NX - 1, send_lo, 0)
 
     def relay(buf, n):
         for k in range(NX):
-            px = turned(x, k, NX)
-            wait(buf.at[pl.ds(0, SLAB - TILE if k == NX - 1 else SLAB)], gat_recv.at[n, px])
-            here = slab(c, px)
-            push(buf.at[here], buf.at[here], swap_send.at[n], swap_recv.at[n], mate)
+            px = turned(x, NX - 1 if k == 0 else k - 1, NX)
+            if k > 0:
+                wait(buf.at[0, 0, 0], gat_recv.at[n, 3 + px])
+            push(buf.at[0, c, px], buf.at[0, c, px], swap_send.at[n], swap_recv.at[n], mate)
+        wait(buf.at[0, 0, :, pl.ds(0, NU - 1)], gat_recv.at[n, 2])
+        push(buf.at[1, c], buf.at[1, c], swap_send.at[n], swap_recv.at[n], mate)
 
     def settle(buf, n):
-        wait(buf.at[pl.ds(0, HALF)], swap_recv.at[n])
-        wait(buf.at[pl.ds(0, HALF - TILE)], gat_send.at[n])
-        wait(buf.at[pl.ds(0, HALF)], swap_send.at[n])
-
-    spread(gat_t, 1)
+        wait(buf.at[:, 0], swap_recv.at[n])
+        wait(buf.at[0, 0, 0, pl.ds(0, NU - 1)], gat_send.at[n, 0])
+        wait(buf.at[0, 0, 0, pl.ds(0, NX - 1)], gat_send.at[n, 1])
+        wait(buf.at[0, 0, :, pl.ds(0, NU - 1)], gat_send.at[n, 2])
+        wait(buf.at[0, 0, pl.ds(0, NX - 1)], gat_send.at[n, 3])
+        wait(buf.at[:, 0], swap_send.at[n])
+
+    open_step(gat_t, 1)
     push(proto_hat, proto_mate, mate_send.at[0], mate_recv.at[0], mate)
     wait(first.at[pl.ds(0, NU - 1)], first_send)
+    spread_step(gat_t, 1)
     relay(gat_t, 1)
     settle(gat_t, 1)
 
     def exponentials(buf, out, temp):
         for k in range(ROWS // 256):
             at = slice(k * 256, (k + 1) * 256)
-            product = lax.dot_general(
-                proto_hat[...], buf[at, :], (((1,), (1,)), ((), ())), preferred_element_type=f32
+            px = k % 2 * 2
+            product = sum(
+                lax.dot_general(
+                    proto_hat[:, h * CUT : (h + 1) * CUT],
+                    buf[h, k // 2, px : px + 2].reshape(256, CUT),
+                    (((1,), (1,)), ((), ())),
+                    preferred_element_type=f32,
+                )
+                for h in range(2)
             )
             out[:, at] = jnp.exp(product * (1.0 / temp))
 
@@ -278,29 +310,27 @@
     exponentials(gat_t, e_t, teacher_temp)
     put(near_src.at[0], sweep(None))
     near_start(0)
-    spread(gat_s, 0, 0, NX * NU // 2)
+    open_step(gat_s, 0)
     near_end(0)
     far_start(0)
-    spread(gat_s, 0, NX * NU // 2)
+    spread_step(gat_s, 0)
     row_scale = row_of(far_end(0))
+    relay(gat_s, 0)
 
     put(near_src.at[1], sweep(row_scale))
     near_start(1)
-    relay(gat_s, 0)
-    near_end(1)
-    far_start(1)
     settle(gat_s, 0)
     exponentials(gat_s, e_s, student_temp)
     put(near_src.at[3], lax.fori_loop(0, PROTOS // BLOCK, student_sum, jnp.zeros((8, ROWS), f32)))
     near_start(3)
+    near_end(1)
+    far_start(1)
+    near_end(3)
+    far_start(3)
     row_scale = row_of(far_end(1))
 
     put(near_src.at[2], sweep(row_scale))
     near_start(2)
-    near_end(3)
-    far_start(3)
-    near_end(2)
-    far_start(2)
     student_scale = row_of(far_end(3) * (1.0 / student_temp))
 
     def scale_block(i, _):
@@ -310,6 +340,8 @@
         return 0
 
     lax.fori_loop(0, PROTOS // BLOCK, scale_block, 0)
+    near_end(2)
+    far_start(2)
     part[...] = far_end(2) * (1.0 / student_temp)
 
     def gradients(core):
@@ -355,8 +387,14 @@
 
     def proto_block(i):
         at = slice(i * 256, (i + 1) * 256)
-        step = jnp.dot(grad[0, at, :], gat_s[:HALF, :], preferred_element_type=f32)
-        step += jnp.dot(grad[1, at, :], gat_s[HALF:, :], preferred_element_type=f32)
+        halves = [
+            sum(
+                jnp.dot(grad[core, at, :], gat_s[h, core].reshape(HALF, CUT), preferred_element_type=f32)
+                for core in range(CORES)
+            )
+            for h in range(2)
+        ]
+        step = jnp.concatenate(halves, axis=1)
         inv = proto_inv[at, 0:1]
         unit = proto_ref[at, :].astype(f32) * inv
         pgrad_ref[at, :] = (step - unit * jnp.sum(unit * step, axis=1, keepdims=True)) * inv
@@ -436,8 +474,8 @@
             pltpu.VMEM((PROTOS, D), bf16),
             pltpu.VMEM((NU, 2 * OWN, D), f32),
             pltpu.VMEM((2, TILE, D), f32),
-            pltpu.VMEM((ROWS, D), bf16),
-            pltpu.VMEM((ROWS, D), bf16),
+            pltpu.VMEM((2, CORES, NX, NU, TILE, CUT), bf16),
+            pltpu.VMEM((2, CORES, NX, NU, TILE, CUT), bf16),
             pltpu.VMEM((PROTOS, D), bf16),
             pltpu.VMEM((PROTOS, LANES), f32),
             pltpu.VMEM((PROTOS, ROWS), f32),
@@ -465,8 +503,8 @@
             dma((3,)),
             dma,
             dma,
-            dma((2,)),
-            dma((2, NX)),
+            dma((2, 4)),
+            dma((2, 3 + NX)),
             dma((2,)),
             dma((2,)),
             dma((SUMS,)),

time: 92.4 us -> 93.7 us (1.014)
  Pallas kernels: 89.9 us -> 91.1 us
    pallas_call x1, Pallas kernels: 89.9 us -> 91.1 us  [on_device(): pl.pallas_call(kernel, out_shape=(jax.ShapeDtypeStruct((OWN, D), f32), ja...]
where the time goes in v4:
time: 93.7 us; the launch traced here: 93.3 us
  Pallas kernels  91.1 us (97%)
  local copies, waits for them, and re-layouts  1.56 us (2%)
    pallas_call x1, Pallas kernels, on_device(): pl.pallas_call(kernel, out_shape=(jax.ShapeDtypeStruct((OWN, D), f32), ja...  91.1 us

profile of v4, /device:TPU:1, one launch (start us, length us, event | category | flops | bytes accessed | tf_op | source)
XLA Modules:
  0.0 93.3 jit_solution(10827975749577917069)
XLA Ops:
  0.6 91.1 %prototype_head.1 = (f32[2,512]{1,0:T(2,128)S(1)}, f32[512,512]{1,0:T(8,128)S(1)}) custom-call(bf16[2,512]{1,0:T(2,128)(2,1)} %student_hbm.1, bf16[2,512]{1,0:T(2,128)(2,1)} %teacher_hbm.1, bf16[512,512]{1,0:T(8,128)(2,1)} %proto_hbm.1), custom_call_target="tpu_custom_call" | custom-call | tf_op jit(solution)/shard_map/prototype_head/pallas_call | solution.py:463
  91.7 0.6 copy.7
  92.3 1.0 %copy.8 = f32[512,512]{1,0:T(8,128)} copy(f32[512,512]{1,0:T(8,128)S(1)} %get-tuple-element.5) | data formatting | bytes 2097152

commit v5 on v4

--- a/solution.py
+++ b/solution.py
@@ -1,5 +1,3 @@
-import functools
-
 import jax
 import jax.numpy as jnp
 from jax import lax
@@ -60,7 +58,6 @@
     far_src,
     far,
     part,
-    own,
     proto_mate,
     grad_mate,
     xbuf,
@@ -86,6 +83,7 @@
     far_recv,
     mate_send,
     mate_recv,
+    grad_recv,
     big_send,
     big_recv,
     end_send,
@@ -227,7 +225,7 @@
         wait(buf.at[:, 0], swap_send.at[n])
 
     open_step(gat_t, 1)
-    push(proto_hat, proto_mate, mate_send.at[0], mate_recv.at[0], mate)
+    push(proto_hat, proto_mate, mate_send.at[0], mate_recv, mate)
     wait(first.at[pl.ds(0, NU - 1)], first_send)
     spread_step(gat_t, 1)
     relay(gat_t, 1)
@@ -315,22 +313,24 @@
     far_start(0)
     spread_step(gat_s, 0)
     row_scale = row_of(far_end(0))
-    relay(gat_s, 0)
 
     put(near_src.at[1], sweep(row_scale))
     near_start(1)
+    relay(gat_s, 0)
+    near_end(1)
+    far_start(1)
     settle(gat_s, 0)
     exponentials(gat_s, e_s, student_temp)
     put(near_src.at[3], lax.fori_loop(0, PROTOS // BLOCK, student_sum, jnp.zeros((8, ROWS), f32)))
     near_start(3)
-    near_end(1)
-    far_start(1)
     near_end(3)
     far_start(3)
     row_scale = row_of(far_end(1))
 
     put(near_src.at[2], sweep(row_scale))
     near_start(2)
+    near_end(2)
+    far_start(2)
     student_scale = row_of(far_end(3) * (1.0 / student_temp))
 
     def scale_block(i, _):
@@ -340,60 +340,56 @@
         return 0
 
     lax.fori_loop(0, PROTOS // BLOCK, scale_block, 0)
-    near_end(2)
-    far_start(2)
     part[...] = far_end(2) * (1.0 / student_temp)
 
-    def gradients(core):
-        rows = [part[pl.ds(core * (TALL // CORES) + k, 1), :] for k in range(TALL // CORES)]
-        scale = jnp.concatenate(rows, axis=1)
-        lanes = pl.ds(pl.multiple_of(core * HALF, HALF), HALF)
+    def gradients(core, px):
+        scale = part[pl.ds(core * NX + px, 1), :]
 
         def body(i, _):
-            at = pl.ds(pl.multiple_of(i * BLOCK, BLOCK), BLOCK)
-            grad[core, at, :] = (e_s[at, lanes] - e_t[at, lanes] * scale).astype(bf16)
-            return 0
-
-        lax.fori_loop(0, PROTOS // BLOCK, body, 0)
-
-    gradients(oc)
-    push(grad.at[oc], grad_mate, mate_send.at[1], mate_recv.at[1], mate)
-    gradients(c)
-
-    def row_product(left, px, right):
-        at = pl.ds(pl.multiple_of(px * SLAB, SLAB), SLAB)
-        return lax.dot_general(left[:, at], right[...], (((0,), (0,)), ((), ())), preferred_element_type=f32)
-
-    for px in range(NX):
-        own[px] = row_product(grad.at[c], px, proto_hat)
-    wait(proto_mate, mate_recv.at[0])
-    wait(grad_mate, mate_recv.at[1])
+            at = pl.ds(pl.multiple_of(i * 128, 128), 128)
+            lanes = pl.ds(pl.multiple_of(core * HALF + px * SLAB, SLAB), SLAB)
+            grad[core, px, at, :] = (e_s[at, lanes] - e_t[at, lanes] * scale).astype(bf16)
+            return 0
+
+        lax.fori_loop(0, PROTOS // 128, body, 0)
+
+    def row_product(left, right):
+        return lax.dot_general(left[...], right[...], (((0,), (0,)), ((), ())), preferred_element_type=f32)
+
     for k in range(NX):
         px = turned(x, k, NX)
-        total = own[px] + row_product(grad_mate, px, proto_mate)
+        gradients(oc, px)
+        push(grad.at[oc, px], grad_mate.at[px], mate_send.at[1], grad_recv.at[px], mate)
+    wait(proto_mate, mate_recv)
+    for k in range(NX):
+        px = turned(x, k, NX)
+        gradients(c, px)
+        own = row_product(grad.at[c, px], proto_hat)
+        wait(grad_mate.at[px], grad_recv.at[px])
+        total = own + row_product(grad_mate.at[px], proto_mate)
         xbuf[px] = total[:, :CUT]
         ubuf[px] = total[:, CUT:].reshape(NU, TILE, D - CUT)
         if k < NX - 1:
             push(xbuf.at[px], xslots.at[x], big_send.at[0], big_recv.at[0], device(px, u, v))
 
-    def send_u(k, _):
-        pu = turned(u, k, NU)
-        push(ubuf.at[:, pu], uslots.at[u], big_send.at[1], big_recv.at[1], device(x, pu, v))
-        return 0
-
-    lax.fori_loop(0, NU - 1, send_u, 0)
+        def send_u(j, _):
+            pu = turned(u, j, NU)
+            push(ubuf.at[px, pu], uslots.at[u, px], big_send.at[1], big_recv.at[1], device(x, pu, v))
+            return 0
+
+        lax.fori_loop(0, NU - 1, send_u, 0)
     xslots[x] = xbuf[x]
     uslots[u] = ubuf[:, u]
 
     def proto_block(i):
         at = slice(i * 256, (i + 1) * 256)
-        halves = [
-            sum(
-                jnp.dot(grad[core, at, :], gat_s[h, core].reshape(HALF, CUT), preferred_element_type=f32)
-                for core in range(CORES)
-            )
-            for h in range(2)
-        ]
+        halves = [0.0, 0.0]
+        for core in range(CORES):
+            for px in range(0, NX, 2):
+                left = jnp.concatenate([grad[core, px, at, :], grad[core, px + 1, at, :]], axis=1)
+                for h in range(2):
+                    right = gat_s[h, core, px : px + 2].reshape(2 * SLAB, CUT)
+                    halves[h] += jnp.dot(left, right, preferred_element_type=f32)
         step = jnp.concatenate(halves, axis=1)
         inv = proto_inv[at, 0:1]
         unit = proto_ref[at, :].astype(f32) * inv
@@ -481,15 +477,14 @@
             pltpu.VMEM((PROTOS, ROWS), f32),
             pltpu.VMEM((PROTOS, ROWS), f32),
             pltpu.VMEM((PROTOS, LANES), f32),
-            pltpu.VMEM((CORES, PROTOS, HALF), bf16),
+            pltpu.VMEM((CORES, NX, PROTOS, SLAB), bf16),
             pltpu.VMEM((SUMS, TALL, LANES), f32),
             pltpu.VMEM((SUMS, NU * CORES, TALL, LANES), f32),
             pltpu.VMEM((SUMS, TALL, LANES), f32),
             pltpu.VMEM((SUMS, NX * NU, TALL, LANES), f32),
             pltpu.VMEM((TALL, LANES), f32),
-            pltpu.VMEM((NX, SLAB, D), f32),
             pltpu.VMEM((PROTOS, D), bf16),
-            pltpu.VMEM((PROTOS, HALF), bf16),
+            pltpu.VMEM((NX, PROTOS, SLAB), bf16),
             pltpu.VMEM((NX, SLAB, CUT), f32),
             pltpu.VMEM((NX, NU, TILE, D - CUT), f32),
             pltpu.VMEM((NX, SLAB, CUT), f32),
@@ -512,7 +507,8 @@
             dma((SUMS,)),
             dma((SUMS,)),
             dma((2,)),
-            dma((2,)),
+            dma,
+            dma((NX,)),
             dma((2,)),
             dma((2,)),
             dma((3,)),

time: 93.7 us -> 94.1 us (level)
  no operation moved by 1% of the time
where the time goes in v5:
time: 94.1 us; the launch traced here: 93.8 us
  Pallas kernels  91.6 us (97%)
  local copies, waits for them, and re-layouts  1.56 us (2%)
    pallas_call x1, Pallas kernels, on_device(): pl.pallas_call(kernel, out_shape=(jax.ShapeDtypeStruct((OWN, D), f32), ja...  91.6 us

profile of v5, /device:TPU:1, one launch (start us, length us, event | category | flops | bytes accessed | tf_op | source)
XLA Modules:
  0.0 93.8 jit_solution(6546679901635406359)
XLA Ops:
  0.6 91.6 %prototype_head.1 = (f32[2,512]{1,0:T(2,128)S(1)}, f32[512,512]{1,0:T(8,128)S(1)}) custom-call(bf16[2,512]{1,0:T(2,128)(2,1)} %student_hbm.1, bf16[2,512]{1,0:T(2,128)(2,1)} %teacher_hbm.1, bf16[512,512]{1,0:T(8,128)(2,1)} %proto_hbm.1), custom_call_target="tpu_custom_call" | custom-call | tf_op jit(solution)/shard_map/prototype_head/pallas_call | solution.py:459
  92.3 0.6 copy.7
  92.9 1.0 %copy.8 = f32[512,512]{1,0:T(8,128)} copy(f32[512,512]{1,0:T(8,128)S(1)} %get-tuple-element.5) | data formatting | bytes 2097152

commit v6 on v4

--- a/solution.py
+++ b/solution.py
@@ -1,5 +1,3 @@
-import functools
-
 import jax
 import jax.numpy as jnp
 from jax import lax
@@ -190,24 +188,30 @@
             push(block, block, gat_send.at[n, 0], gat_recv.at[n, 0], device(x, turned(u, k, NU), v))
             return 0
 
+        lax.fori_loop(0, NX - 1, send_hi, 0)
         lax.fori_loop(0, NU - 1, send_lo, 0)
-        lax.fori_loop(0, NX - 1, send_hi, 0)
-
-    def spread_step(buf, n):
-        def send_hi(k, _):
+
+    def spread_hi(buf, n):
+        def send(k, _):
             block = buf.at[1, c, :, u]
             push(block, block, gat_send.at[n, 2], gat_recv.at[n, 2], device(x, turned(u, k, NU), v))
             return 0
 
-        def send_lo(k, _):
+        lax.fori_loop(0, NU - 1, send, 0)
+
+    def spread_lo(buf, n):
+        def send(k, _):
             block = buf.at[0, c, x]
             push(block, block, gat_send.at[n, 3], gat_recv.at[n, 3 + x], device(turned(x, k, NX), u, v))
             return 0
 
+        lax.fori_loop(0, NX - 1, send, 0)
+
+    def opened_hi(buf, n):
         wait(buf.at[0, 0, 0, pl.ds(0, NX - 1)], gat_recv.at[n, 1])
-        lax.fori_loop(0, NU - 1, send_hi, 0)
+
+    def opened_lo(buf, n):
         wait(buf.at[0, 0, 0, pl.ds(0, NU - 1)], gat_recv.at[n, 0])
-        lax.fori_loop(0, NX - 1, send_lo, 0)
 
     def relay(buf, n):
         for k in range(NX):
@@ -229,7 +233,11 @@
     open_step(gat_t, 1)
     push(proto_hat, proto_mate, mate_send.at[0], mate_recv.at[0], mate)
     wait(first.at[pl.ds(0, NU - 1)], first_send)
-    spread_step(gat_t, 1)
+    opened_hi(gat_t, 1)
+    spread_hi(gat_t, 1)
+    opened_lo(gat_t, 1)
+    spread_lo(gat_t, 1)
+    open_step(gat_s, 0)
     relay(gat_t, 1)
     settle(gat_t, 1)
 
@@ -310,10 +318,13 @@
     exponentials(gat_t, e_t, teacher_temp)
     put(near_src.at[0], sweep(None))
     near_start(0)
-    open_step(gat_s, 0)
+    opened_hi(gat_s, 0)
+    opened_lo(gat_s, 0)
+    spread_lo(gat_s, 0)
+    pl.when(c == 1)(lambda: spread_hi(gat_s, 0))
     near_end(0)
     far_start(0)
-    spread_step(gat_s, 0)
+    pl.when(c == 0)(lambda: spread_hi(gat_s, 0))
     row_scale = row_of(far_end(0))
     relay(gat_s, 0)
 

time: 93.7 us -> 93.2 us (level)
  no operation moved by 1% of the time
where the time goes in v6:
time: 93.2 us; the launch traced here: 92.6 us
  Pallas kernels  90.4 us (97%)
  local copies, waits for them, and re-layouts  1.56 us (2%)
    pallas_call x1, Pallas kernels, on_device(): pl.pallas_call(kernel, out_shape=(jax.ShapeDtypeStruct((OWN, D), f32), ja...  90.4 us

profile of v6, /device:TPU:1, one launch (start us, length us, event | category | flops | bytes accessed | tf_op | source)
XLA Modules:
  0.0 92.6 jit_solution(9601166612345920264)
XLA Ops:
  0.6 90.4 %prototype_head.1 = (f32[2,512]{1,0:T(2,128)S(1)}, f32[512,512]{1,0:T(8,128)S(1)}) custom-call(bf16[2,512]{1,0:T(2,128)(2,1)} %student_hbm.1, bf16[2,512]{1,0:T(2,128)(2,1)} %teacher_hbm.1, bf16[512,512]{1,0:T(8,128)(2,1)} %proto_hbm.1), custom_call_target="tpu_custom_call" | custom-call | tf_op jit(solution)/shard_map/prototype_head/pallas_call | solution.py:474
  91.0 0.6 copy.7
  91.6 1.0 %copy.8 = f32[512,512]{1,0:T(8,128)} copy(f32[512,512]{1,0:T(8,128)S(1)} %get-tuple-element.5) | data formatting | bytes 2097152

commit v7 on v6

--- a/solution.py
+++ b/solution.py
@@ -8,7 +8,7 @@
 
 MESH = pl.DeviceIdType.MESH
 AXES = ("wide_0", "wide_1", "narrow_0", "narrow_1")
-SUMS = 4
+SUMS = 3
 NX, NU, CORES = 4, 8, 2
 D = 512
 OWN = 2
@@ -67,10 +67,16 @@
     uslots,
     xsum,
     xuslots,
-    xvsrc,
-    xvslots,
-    uvsrc,
-    uvslots,
+    uxsrc,
+    uxslots,
+    vsrc,
+    vslots,
+    st_src,
+    st_near,
+    st_part,
+    st_far,
+    st_tot,
+    st_all,
     load,
     first_send,
     first_recv,
@@ -88,6 +94,8 @@
     big_recv,
     end_send,
     end_recv,
+    st_send,
+    st_recv,
 ):
     x, y, z, c = (lax.axis_index(a) for a in AXES)
     u = z + c * (y - z)
@@ -107,9 +115,6 @@
 
     def far_peer(k):
         return (turned(x, lax.rem(k, NX), NX), turned(y, k // NX, NU), z, c)
-
-    def plane(k, at):
-        return turned(x, lax.rem(k, NX), NX), turned(at, k // NX, NU)
 
     def wait(ref, sem):
         pltpu.make_async_copy(ref, ref, sem).wait()
@@ -134,11 +139,7 @@
         pl.semaphore_signal(barrier, inc=1, device_id=target, device_id_type=MESH)
         return 0
 
-    def greet_side(k, _):
-        return greet((turned(x, lax.rem(k, NX - 1), NX), y, turned(z, k // (NX - 1), NU), c))
-
     lax.fori_loop(0, NX * NU - 1, lambda k, _: greet(far_peer(k)), 0)
-    lax.fori_loop(0, (NX - 1) * (NU - 1), greet_side, 0)
     lax.fori_loop(0, NU * CORES - 1, lambda k, _: greet(near_peer(k)), 0)
 
     for copy in inputs[:2]:
@@ -159,7 +160,7 @@
         proto_hat[at, :] = (wide * inv).astype(bf16)
         return 0
 
-    pl.semaphore_wait(barrier, NU * CORES - 1 + NX * NU - 1 + (NX - 1) * (NU - 1))
+    pl.semaphore_wait(barrier, NU * CORES - 1 + NX * NU - 1)
 
     def send_first(k, _):
         push(first.at[v], first.at[v], first_send, first_recv, device(x, u, turned(v, k, NU)))
@@ -326,23 +327,53 @@
     far_start(0)
     pl.when(c == 0)(lambda: spread_hi(gat_s, 0))
     row_scale = row_of(far_end(0))
-    relay(gat_s, 0)
 
     put(near_src.at[1], sweep(row_scale))
     near_start(1)
+    relay(gat_s, 0)
+    near_end(1)
+    far_start(1)
     settle(gat_s, 0)
     exponentials(gat_s, e_s, student_temp)
-    put(near_src.at[3], lax.fori_loop(0, PROTOS // BLOCK, student_sum, jnp.zeros((8, ROWS), f32)))
-    near_start(3)
-    near_end(1)
-    far_start(1)
-    near_end(3)
-    far_start(3)
+    student_part = lax.fori_loop(0, PROTOS // BLOCK, student_sum, jnp.zeros((8, ROWS), f32))
+    for k in range(TALL):
+        st_src[k] = jnp.sum(student_part[:, k * LANES : (k + 1) * LANES], axis=0, keepdims=True)
+
+    def send_piece(k, _):
+        pz = turned(z, k, NU)
+        push(st_src.at[pz], st_near.at[z], st_send.at[0], st_recv.at[0], (x, y, pz, c))
+        return 0
+
+    def send_sum(k, _):
+        push(st_part, st_far.at[x * NU + y], st_send.at[1], st_recv.at[1], far_peer(k))
+        return 0
+
+    def send_back(k, _):
+        push(st_tot, st_all.at[z * CORES + c], st_send.at[2], st_recv.at[2], near_peer(k))
+        return 0
+
+    lax.fori_loop(0, NU - 1, send_piece, 0)
+    st_near[z] = st_src[z]
+    for sem in (st_recv, st_send):
+        wait(st_near.at[pl.ds(0, NU - 1)], sem.at[0])
+    st_part[...] = jnp.sum(st_near[...], axis=0)
+    lax.fori_loop(0, NX * NU - 1, send_sum, 0)
+    st_far[x * NU + y] = st_part[...]
     row_scale = row_of(far_end(1))
 
     put(near_src.at[2], sweep(row_scale))
     near_start(2)
-    student_scale = row_of(far_end(3) * (1.0 / student_temp))
+    near_end(2)
+    far_start(2)
+    for sem in (st_recv, st_send):
+        wait(st_far.at[pl.ds(0, NX * NU - 1)], sem.at[1])
+    st_tot[...] = jnp.sum(st_far[...], axis=0)
+    lax.fori_loop(0, NU * CORES - 1, send_back, 0)
+    st_all[z * CORES + c] = st_tot[...]
+    for sem in (st_recv, st_send):
+        wait(st_all.at[pl.ds(0, NU * CORES - 1)], sem.at[2])
+    totals = [st_all[CORES * k] + st_all[CORES * k + 1] for k in range(TALL)]
+    student_scale = (1.0 / jnp.concatenate(totals, axis=1)) * (1.0 / student_temp)
 
     def scale_block(i, _):
         at = pl.ds(pl.multiple_of(i * BLOCK, BLOCK), BLOCK)
@@ -351,8 +382,6 @@
         return 0
 
     lax.fori_loop(0, PROTOS // BLOCK, scale_block, 0)
-    near_end(2)
-    far_start(2)
     part[...] = far_end(2) * (1.0 / student_temp)
 
     def gradients(core):
@@ -428,43 +457,40 @@
 
     for sem in (big_recv, big_send):
         wait(uslots.at[pl.ds(0, NU - 1)], sem.at[1])
-    usum = jnp.sum(uslots[...], axis=0)
-    for px in range(NX):
-        for pv in range(NU):
-            uvsrc[px * NU + pv] = usum[px, pv * OWN : (pv + 1) * OWN, :]
-
-    def send_uv(k, _):
-        px, pv = plane(k, v)
-        push(uvsrc.at[px * NU + pv], uvslots.at[x * NU + v], end_send.at[1], end_recv.at[1], device(px, u, pv))
-        return 0
-
-    lax.fori_loop(0, NX * NU - 1, send_uv, 0)
-    uvslots[x * NU + v] = uvsrc[x * NU + v]
+    uxsrc[...] = jnp.sum(uslots[...], axis=0)
+
+    def send_ux(k, _):
+        px = turned(x, k, NX)
+        push(uxsrc.at[px], uxslots.at[x], end_send.at[1], end_recv.at[1], device(px, u, v))
+        return 0
+
+    lax.fori_loop(0, NX - 1, send_ux, 0)
+    uxslots[x] = uxsrc[x]
 
     for sem in (end_recv, end_send):
         wait(xuslots.at[pl.ds(0, NU - 1)], sem.at[0])
-    xusum = jnp.sum(xuslots[...], axis=0)
+    left = jnp.sum(xuslots[...], axis=0)
+    for sem in (end_recv, end_send):
+        wait(uxslots.at[pl.ds(0, NX - 1)], sem.at[1])
+    right = jnp.sum(uxslots[...], axis=0)
     for pv in range(NU):
-        xvsrc[pv] = xusum[pv * OWN : (pv + 1) * OWN, :]
-
-    def send_xv(k, _):
+        at = slice(pv * OWN, (pv + 1) * OWN)
+        vsrc[pv, :, :CUT] = left[at, :]
+        vsrc[pv, :, CUT:] = right[at, :]
+
+    def send_v(k, _):
         pv = turned(v, k, NU)
-        push(xvsrc.at[pv], xvslots.at[v], end_send.at[2], end_recv.at[2], device(x, u, pv))
-        return 0
-
-    lax.fori_loop(0, NU - 1, send_xv, 0)
-    xvslots[v] = xvsrc[v]
-
+        push(vsrc.at[pv], vslots.at[v], end_send.at[2], end_recv.at[2], device(x, u, pv))
+        return 0
+
+    lax.fori_loop(0, NU - 1, send_v, 0)
+    vslots[v] = vsrc[v]
     for sem in (end_recv, end_send):
-        wait(uvslots.at[pl.ds(0, NX * NU - 1)], sem.at[1])
-    right = jnp.sum(uvslots[...], axis=0)
-    for sem in (end_recv, end_send):
-        wait(xvslots.at[pl.ds(0, NU - 1)], sem.at[2])
-    left = jnp.sum(xvslots[...], axis=0)
+        wait(vslots.at[pl.ds(0, NU - 1)], sem.at[2])
+    step = jnp.sum(vslots[...], axis=0)
     wait(proto_mate, mate_send.at[0])
     wait(grad_mate, mate_send.at[1])
 
-    step = jnp.concatenate([left, right], axis=1)
     sgrad_ref[...] = (step - s_unit * jnp.sum(s_unit * step, axis=1, keepdims=True)) * s_inv
 
 
@@ -507,10 +533,16 @@
             pltpu.VMEM((NU, NX, TILE, D - CUT), f32),
             pltpu.VMEM((SLAB, CUT), f32),
             pltpu.VMEM((NU, TILE, CUT), f32),
-            pltpu.VMEM((NU, OWN, CUT), f32),
-            pltpu.VMEM((NU, OWN, CUT), f32),
-            pltpu.VMEM((NX * NU, OWN, D - CUT), f32),
-            pltpu.VMEM((NX * NU, OWN, D - CUT), f32),
+            pltpu.VMEM((NX, TILE, D - CUT), f32),
+            pltpu.VMEM((NX, TILE, D - CUT), f32),
+            pltpu.VMEM((NU, OWN, D), f32),
+            pltpu.VMEM((NU, OWN, D), f32),
+            pltpu.VMEM((TALL, 1, LANES), f32),
+            pltpu.VMEM((NU, 1, LANES), f32),
+            pltpu.VMEM((1, LANES), f32),
+            pltpu.VMEM((NX * NU, 1, LANES), f32),
+            pltpu.VMEM((1, LANES), f32),
+            pltpu.VMEM((NU * CORES, 1, LANES), f32),
             dma((3,)),
             dma,
             dma,
@@ -528,6 +560,8 @@
             dma((2,)),
             dma((3,)),
             dma((3,)),
+            dma((3,)),
+            dma((3,)),
         ],
         compiler_params=pltpu.CompilerParams(
             collective_id=0, has_side_effects=True, vmem_limit_bytes=48 << 20

time: 93.2 us -> 91.6 us (0.983)
  Pallas kernels: 90.4 us -> 89.2 us
    pallas_call x1, Pallas kernels: 90.4 us -> 89.2 us  [on_device(): pl.pallas_call(kernel, out_shape=(jax.ShapeDtypeStruct((OWN, D), f32), ja...]
where the time goes in v7:
time: 91.6 us; the launch traced here: 91.4 us
  Pallas kernels  89.2 us (97%)
  local copies, waits for them, and re-layouts  1.56 us (2%)
    pallas_call x1, Pallas kernels, on_device(): pl.pallas_call(kernel, out_shape=(jax.ShapeDtypeStruct((OWN, D), f32), ja...  89.2 us

profile of v7, /device:TPU:1, one launch (start us, length us, event | category | flops | bytes accessed | tf_op | source)
XLA Modules:
  0.0 91.4 jit_solution(3781694365575234466)
XLA Ops:
  0.6 89.2 %prototype_head.1 = (f32[2,512]{1,0:T(2,128)S(1)}, f32[512,512]{1,0:T(8,128)S(1)}) custom-call(bf16[2,512]{1,0:T(2,128)(2,1)} %student_hbm.1, bf16[2,512]{1,0:T(2,128)(2,1)} %teacher_hbm.1, bf16[512,512]{1,0:T(8,128)(2,1)} %proto_hbm.1), custom_call_target="tpu_custom_call" | custom-call | tf_op jit(solution)/shard_map/prototype_head/pallas_call | solution.py:500
  89.9 0.6 copy.7
  90.5 1.0 %copy.8 = f32[512,512]{1,0:T(8,128)} copy(f32[512,512]{1,0:T(8,128)S(1)} %get-tuple-element.5) | data formatting | bytes 2097152

commit v8 on v7

--- a/solution.py
+++ b/solution.py
@@ -17,7 +17,7 @@
 SLAB = HALF // NX
 TILE = NU * OWN
 PROTOS = 512
-BLOCK = 64
+BLOCK = 128
 LANES = 128
 TALL = ROWS // LANES
 CUT = D // 2
@@ -28,6 +28,10 @@
 
 f32 = jnp.float32
 bf16 = jnp.bfloat16
+
+
+def rem(k, n):
+    return k % n if isinstance(k, int) else lax.rem(k, n)
 
 
 def inverse_norm(wide):
@@ -108,13 +112,13 @@
     mate = (x, y, z, oc)
 
     def turned(at, k, n):
-        return lax.rem(at + n // 2 + (1 - 2 * lax.rem(k, 2)) * ((k + 1) // 2), n)
+        return lax.rem(at + (n // 2 + (1 - 2 * rem(k, 2)) * ((k + 1) // 2)), n)
 
     def near_peer(k):
-        return (x, y, turned(z, k // CORES, NU), lax.rem(c + 1 + lax.rem(k, CORES), CORES))
+        return (x, y, turned(z, k // CORES, NU), lax.rem(c + (1 + rem(k, CORES)), CORES))
 
     def far_peer(k):
-        return (turned(x, lax.rem(k, NX), NX), turned(y, k // NX, NU), z, c)
+        return (turned(x, rem(k, NX), NX), turned(y, k // NX, NU), z, c)
 
     def wait(ref, sem):
         pltpu.make_async_copy(ref, ref, sem).wait()
@@ -137,10 +141,11 @@
 
     def greet(target):
         pl.semaphore_signal(barrier, inc=1, device_id=target, device_id_type=MESH)
-        return 0
-
-    lax.fori_loop(0, NX * NU - 1, lambda k, _: greet(far_peer(k)), 0)
-    lax.fori_loop(0, NU * CORES - 1, lambda k, _: greet(near_peer(k)), 0)
+
+    for k in range(NX * NU - 1):
+        greet(far_peer(k))
+    for k in range(NU * CORES - 1):
+        greet(near_peer(k))
 
     for copy in inputs[:2]:
         copy.wait()
@@ -232,7 +237,6 @@
         wait(buf.at[:, 0], swap_send.at[n])
 
     open_step(gat_t, 1)
-    push(proto_hat, proto_mate, mate_send.at[0], mate_recv.at[0], mate)
     wait(first.at[pl.ds(0, NU - 1)], first_send)
     opened_hi(gat_t, 1)
     spread_hi(gat_t, 1)
@@ -240,16 +244,15 @@
     spread_lo(gat_t, 1)
     open_step(gat_s, 0)
     relay(gat_t, 1)
-    settle(gat_t, 1)
-
-    def exponentials(buf, out, temp):
-        for k in range(ROWS // 256):
-            at = slice(k * 256, (k + 1) * 256)
-            px = k % 2 * 2
+
+    def exponentials(buf, out, temp, core):
+        for k in range(HALF // 256):
+            at = pl.ds(pl.multiple_of(core * HALF + k * 256, 256), 256)
+            px = k * 256 // SLAB
             product = sum(
                 lax.dot_general(
                     proto_hat[:, h * CUT : (h + 1) * CUT],
-                    buf[h, k // 2, px : px + 2].reshape(256, CUT),
+                    buf[h, core, px : px + 256 // SLAB].reshape(256, CUT),
                     (((1,), (1,)), ((), ())),
                     preferred_element_type=f32,
                 )
@@ -316,9 +319,12 @@
         at = pl.ds(pl.multiple_of(i * BLOCK, BLOCK), BLOCK)
         return acc + folded(e_s[at, :])
 
-    exponentials(gat_t, e_t, teacher_temp)
+    exponentials(gat_t, e_t, teacher_temp, c)
+    settle(gat_t, 1)
+    exponentials(gat_t, e_t, teacher_temp, oc)
     put(near_src.at[0], sweep(None))
     near_start(0)
+    push(proto_hat, proto_mate, mate_send.at[0], mate_recv.at[0], mate)
     opened_hi(gat_s, 0)
     opened_lo(gat_s, 0)
     spread_lo(gat_s, 0)
@@ -334,7 +340,8 @@
     near_end(1)
     far_start(1)
     settle(gat_s, 0)
-    exponentials(gat_s, e_s, student_temp)
+    for core in range(CORES):
+        exponentials(gat_s, e_s, student_temp, core)
     student_part = lax.fori_loop(0, PROTOS // BLOCK, student_sum, jnp.zeros((8, ROWS), f32))
     for k in range(TALL):
         st_src[k] = jnp.sum(student_part[:, k * LANES : (k + 1) * LANES], axis=0, keepdims=True)

time: 91.6 us -> 89.7 us (0.979)
  Pallas kernels: 89.2 us -> 87.4 us
    pallas_call x1, Pallas kernels: 89.2 us -> 87.4 us  [on_device(): pl.pallas_call(kernel, out_shape=(jax.ShapeDtypeStruct((OWN, D), f32), ja...]
where the time goes in v8:
time: 89.7 us; the launch traced here: 89.6 us
  Pallas kernels  87.4 us (97%)
  local copies, waits for them, and re-layouts  1.56 us (2%)
    pallas_call x1, Pallas kernels, on_device(): pl.pallas_call(kernel, out_shape=(jax.ShapeDtypeStruct((OWN, D), f32), ja...  87.4 us

profile of v8, /device:TPU:1, one launch (start us, length us, event | category | flops | bytes accessed | tf_op | source)
XLA Modules:
  0.0 89.6 jit_solution(4660718817672675696)
XLA Ops:
  0.6 87.4 %prototype_head.1 = (f32[2,512]{1,0:T(2,128)S(1)}, f32[512,512]{1,0:T(8,128)S(1)}) custom-call(bf16[2,512]{1,0:T(2,128)(2,1)} %student_hbm.1, bf16[2,512]{1,0:T(2,128)(2,1)} %teacher_hbm.1, bf16[512,512]{1,0:T(8,128)(2,1)} %proto_hbm.1), custom_call_target="tpu_custom_call" | custom-call | tf_op jit(solution)/shard_map/prototype_head/pallas_call | solution.py:507
  88.0 0.6 copy.7
  88.6 1.0 %copy.8 = f32[512,512]{1,0:T(8,128)} copy(f32[512,512]{1,0:T(8,128)S(1)} %get-tuple-element.5) | data formatting | bytes 2097152

commit v9 on v8

--- a/solution.py
+++ b/solution.py
@@ -18,6 +18,7 @@
 TILE = NU * OWN
 PROTOS = 512
 BLOCK = 128
+SWEEP = 256
 LANES = 128
 TALL = ROWS // LANES
 CUT = D // 2
@@ -30,8 +31,9 @@
 bf16 = jnp.bfloat16
 
 
-def rem(k, n):
-    return k % n if isinstance(k, int) else lax.rem(k, n)
+def each(n, act):
+    for k in range(n):
+        act(k)
 
 
 def inverse_norm(wide):
@@ -112,13 +114,13 @@
     mate = (x, y, z, oc)
 
     def turned(at, k, n):
-        return lax.rem(at + (n // 2 + (1 - 2 * rem(k, 2)) * ((k + 1) // 2)), n)
+        return lax.rem(at + (n // 2 + (1 - 2 * (k % 2)) * ((k + 1) // 2)), n)
 
     def near_peer(k):
-        return (x, y, turned(z, k // CORES, NU), lax.rem(c + (1 + rem(k, CORES)), CORES))
+        return (x, y, turned(z, k // CORES, NU), lax.rem(c + (1 + k % CORES), CORES))
 
     def far_peer(k):
-        return (turned(x, rem(k, NX), NX), turned(y, k // NX, NU), z, c)
+        return (turned(x, k % NX, NX), turned(y, k // NX, NU), z, c)
 
     def wait(ref, sem):
         pltpu.make_async_copy(ref, ref, sem).wait()
@@ -142,10 +144,8 @@
     def greet(target):
         pl.semaphore_signal(barrier, inc=1, device_id=target, device_id_type=MESH)
 
-    for k in range(NX * NU - 1):
-        greet(far_peer(k))
-    for k in range(NU * CORES - 1):
-        greet(near_peer(k))
+    each(NX * NU - 1, lambda k: greet(far_peer(k)))
+    each(NU * CORES - 1, lambda k: greet(near_peer(k)))
 
     for copy in inputs[:2]:
         copy.wait()
@@ -167,11 +167,10 @@
 
     pl.semaphore_wait(barrier, NU * CORES - 1 + NX * NU - 1)
 
-    def send_first(k, _):
+    def send_first(k):
         push(first.at[v], first.at[v], first_send, first_recv, device(x, u, turned(v, k, NU)))
-        return 0
-
-    lax.fori_loop(0, NU - 1, send_first, 0)
+
+    each(NU - 1, send_first)
     inputs[2].wait()
     lax.fori_loop(0, PROTOS // BLOCK, norm_block, 0)
     wait(first.at[pl.ds(0, NU - 1)], first_recv)
@@ -184,34 +183,30 @@
         gat_t[h, c, x, u] = stage[1, :, at].astype(bf16)
 
     def open_step(buf, n):
-        def send_hi(k, _):
+        def send_hi(k):
             block = buf.at[1, c, x, u]
             push(block, block, gat_send.at[n, 1], gat_recv.at[n, 1], device(turned(x, k, NX), u, v))
-            return 0
-
-        def send_lo(k, _):
+
+        def send_lo(k):
             block = buf.at[0, c, x, u]
             push(block, block, gat_send.at[n, 0], gat_recv.at[n, 0], device(x, turned(u, k, NU), v))
-            return 0
-
-        lax.fori_loop(0, NX - 1, send_hi, 0)
-        lax.fori_loop(0, NU - 1, send_lo, 0)
+
+        each(NX - 1, send_hi)
+        each(NU - 1, send_lo)
 
     def spread_hi(buf, n):
-        def send(k, _):
+        def send(k):
             block = buf.at[1, c, :, u]
             push(block, block, gat_send.at[n, 2], gat_recv.at[n, 2], device(x, turned(u, k, NU), v))
-            return 0
-
-        lax.fori_loop(0, NU - 1, send, 0)
+
+        each(NU - 1, send)
 
     def spread_lo(buf, n):
-        def send(k, _):
+        def send(k):
             block = buf.at[0, c, x]
             push(block, block, gat_send.at[n, 3], gat_recv.at[n, 3 + x], device(turned(x, k, NX), u, v))
-            return 0
-
-        lax.fori_loop(0, NX - 1, send, 0)
+
+        each(NX - 1, send)
 
     def opened_hi(buf, n):
         wait(buf.at[0, 0, 0, pl.ds(0, NX - 1)], gat_recv.at[n, 1])
@@ -261,7 +256,7 @@
             out[:, at] = jnp.exp(product * (1.0 / temp))
 
     def folded(value):
-        return jnp.sum(value.reshape(BLOCK // 8, 8, ROWS), axis=0)
+        return jnp.sum(value.reshape(-1, 8, ROWS), axis=0)
 
     def flat(ref):
         return jnp.concatenate([ref[k : k + 1, :] for k in range(TALL)], axis=1)
@@ -272,23 +267,22 @@
 
     def sweep(scale):
         def body(i, acc):
-            at = pl.ds(pl.multiple_of(i * BLOCK, BLOCK), BLOCK)
+            at = pl.ds(pl.multiple_of(i * SWEEP, SWEEP), SWEEP)
             e = e_t[at, :]
             weighed = e if scale is None else e * scale
             col = 1.0 / jnp.sum(weighed, axis=1, keepdims=True)
-            cols[at, :] = jnp.broadcast_to(col, (BLOCK, LANES))
+            cols[at, :] = jnp.broadcast_to(col, (SWEEP, LANES))
             return acc + folded(e * col)
 
-        return lax.fori_loop(0, PROTOS // BLOCK, body, jnp.zeros((8, ROWS), f32))
+        return lax.fori_loop(0, PROTOS // SWEEP, body, jnp.zeros((8, ROWS), f32))
 
     def near_start(n):
         me = z * CORES + c
 
-        def send(k, _):
+        def send(k):
             push(near_src.at[n], near.at[n, me], near_send.at[n], near_recv.at[n], near_peer(k))
-            return 0
-
-        lax.fori_loop(0, NU * CORES - 1, send, 0)
+
+        each(NU * CORES - 1, send)
         near[n, me] = near_src[n]
 
     def near_end(n):
@@ -299,11 +293,10 @@
     def far_start(n):
         me = x * NU + y
 
-        def send(k, _):
+        def send(k):
             push(far_src.at[n], far.at[n, me], far_send.at[n], far_recv.at[n], far_peer(k))
-            return 0
-
-        lax.fori_loop(0, NX * NU - 1, send, 0)
+
+        each(NX * NU - 1, send)
         far[n, me] = far_src[n]
 
     def far_end(n):
@@ -346,25 +339,22 @@
     for k in range(TALL):
         st_src[k] = jnp.sum(student_part[:, k * LANES : (k + 1) * LANES], axis=0, keepdims=True)
 
-    def send_piece(k, _):
+    def send_piece(k):
         pz = turned(z, k, NU)
         push(st_src.at[pz], st_near.at[z], st_send.at[0], st_recv.at[0], (x, y, pz, c))
-        return 0
-
-    def send_sum(k, _):
+
+    def send_sum(k):
         push(st_part, st_far.at[x * NU + y], st_send.at[1], st_recv.at[1], far_peer(k))
-        return 0
-
-    def send_back(k, _):
+
+    def send_back(k):
         push(st_tot, st_all.at[z * CORES + c], st_send.at[2], st_recv.at[2], near_peer(k))
-        return 0
-
-    lax.fori_loop(0, NU - 1, send_piece, 0)
+
+    each(NU - 1, send_piece)
     st_near[z] = st_src[z]
     for sem in (st_recv, st_send):
         wait(st_near.at[pl.ds(0, NU - 1)], sem.at[0])
     st_part[...] = jnp.sum(st_near[...], axis=0)
-    lax.fori_loop(0, NX * NU - 1, send_sum, 0)
+    each(NX * NU - 1, send_sum)
     st_far[x * NU + y] = st_part[...]
     row_scale = row_of(far_end(1))
 
@@ -375,7 +365,7 @@
     for sem in (st_recv, st_send):
         wait(st_far.at[pl.ds(0, NX * NU - 1)], sem.at[1])
     st_tot[...] = jnp.sum(st_far[...], axis=0)
-    lax.fori_loop(0, NU * CORES - 1, send_back, 0)
+    each(NU * CORES - 1, send_back)
     st_all[z * CORES + c] = st_tot[...]
     for sem in (st_recv, st_send):
         wait(st_all.at[pl.ds(0, NU * CORES - 1)], sem.at[2])
@@ -423,12 +413,11 @@
         if k < NX - 1:
             push(xbuf.at[px], xslots.at[x], big_send.at[0], big_recv.at[0], device(px, u, v))
 
-    def send_u(k, _):
+    def send_u(k):
         pu = turned(u, k, NU)
         push(ubuf.at[:, pu], uslots.at[u], big_send.at[1], big_recv.at[1], device(x, pu, v))
-        return 0
-
-    lax.fori_loop(0, NU - 1, send_u, 0)
+
+    each(NU - 1, send_u)
     xslots[x] = xbuf[x]
     uslots[u] = ubuf[:, u]
 
@@ -453,25 +442,23 @@
         wait(xslots.at[pl.ds(0, NX - 1)], sem.at[0])
     xsum[...] = jnp.sum(xslots[...], axis=0)
 
-    def send_xu(k, _):
+    def send_xu(k):
         pu = turned(u, k, NU)
         src = xsum.at[pl.ds(pl.multiple_of(pu * TILE, TILE), TILE)]
         push(src, xuslots.at[u], end_send.at[0], end_recv.at[0], device(x, pu, v))
-        return 0
-
-    lax.fori_loop(0, NU - 1, send_xu, 0)
+
+    each(NU - 1, send_xu)
     xuslots[u] = xsum[pl.ds(pl.multiple_of(u * TILE, TILE), TILE), :]
 
     for sem in (big_recv, big_send):
         wait(uslots.at[pl.ds(0, NU - 1)], sem.at[1])
     uxsrc[...] = jnp.sum(uslots[...], axis=0)
 
-    def send_ux(k, _):
+    def send_ux(k):
         px = turned(x, k, NX)
         push(uxsrc.at[px], uxslots.at[x], end_send.at[1], end_recv.at[1], device(px, u, v))
-        return 0
-
-    lax.fori_loop(0, NX - 1, send_ux, 0)
+
+    each(NX - 1, send_ux)
     uxslots[x] = uxsrc[x]
 
     for sem in (end_recv, end_send):
@@ -485,12 +472,11 @@
         vsrc[pv, :, :CUT] = left[at, :]
         vsrc[pv, :, CUT:] = right[at, :]
 
-    def send_v(k, _):
+    def send_v(k):
         pv = turned(v, k, NU)
         push(vsrc.at[pv], vslots.at[v], end_send.at[2], end_recv.at[2], device(x, u, pv))
-        return 0
-
-    lax.fori_loop(0, NU - 1, send_v, 0)
+
+    each(NU - 1, send_v)
     vslots[v] = vsrc[v]
     for sem in (end_recv, end_send):
         wait(vslots.at[pl.ds(0, NU - 1)], sem.at[2])

time: 89.7 us -> 87.6 us (0.977)
  Pallas kernels: 87.4 us -> 85.2 us
    pallas_call x1, Pallas kernels: 87.4 us -> 85.2 us  [on_device(): pl.pallas_call(kernel, out_shape=(jax.ShapeDtypeStruct((OWN, D), f32), ja...]
where the time goes in v9:
time: 87.6 us; the launch traced here: 87.4 us
  Pallas kernels  85.2 us (97%)
  local copies, waits for them, and re-layouts  1.56 us (2%)
    pallas_call x1, Pallas kernels, on_device(): pl.pallas_call(kernel, out_shape=(jax.ShapeDtypeStruct((OWN, D), f32), ja...  85.2 us

profile of v9, /device:TPU:1, one launch (start us, length us, event | category | flops | bytes accessed | tf_op | source)
XLA Modules:
  0.0 87.4 jit_solution(12236832779451636458)
XLA Ops:
  0.6 85.2 %prototype_head.1 = (f32[2,512]{1,0:T(2,128)S(1)}, f32[512,512]{1,0:T(8,128)S(1)}) custom-call(bf16[2,512]{1,0:T(2,128)(2,1)} %student_hbm.1, bf16[2,512]{1,0:T(2,128)(2,1)} %teacher_hbm.1, bf16[512,512]{1,0:T(8,128)(2,1)} %proto_hbm.1), custom_call_target="tpu_custom_call" | custom-call | tf_op jit(solution)/shard_map/prototype_head/pallas_call | solution.py:493
  85.8 0.6 copy.7
  86.4 1.0 %copy.8 = f32[512,512]{1,0:T(8,128)} copy(f32[512,512]{1,0:T(8,128)S(1)} %get-tuple-element.5) | data formatting | bytes 2097152

commit v10 on v9

--- a/solution.py
+++ b/solution.py
@@ -64,7 +64,6 @@
     far_src,
     far,
     part,
-    own,
     proto_mate,
     grad_mate,
     xbuf,
@@ -96,6 +95,7 @@
     far_recv,
     mate_send,
     mate_recv,
+    grad_recv,
     big_send,
     big_recv,
     end_send,
@@ -317,7 +317,7 @@
     exponentials(gat_t, e_t, teacher_temp, oc)
     put(near_src.at[0], sweep(None))
     near_start(0)
-    push(proto_hat, proto_mate, mate_send.at[0], mate_recv.at[0], mate)
+    push(proto_hat, proto_mate, mate_send.at[0], mate_recv, mate)
     opened_hi(gat_s, 0)
     opened_lo(gat_s, 0)
     spread_lo(gat_s, 0)
@@ -381,33 +381,25 @@
     lax.fori_loop(0, PROTOS // BLOCK, scale_block, 0)
     part[...] = far_end(2) * (1.0 / student_temp)
 
-    def gradients(core):
-        rows = [part[pl.ds(core * (TALL // CORES) + k, 1), :] for k in range(TALL // CORES)]
-        scale = jnp.concatenate(rows, axis=1)
-        lanes = pl.ds(pl.multiple_of(core * HALF, HALF), HALF)
-
-        def body(i, _):
-            at = pl.ds(pl.multiple_of(i * BLOCK, BLOCK), BLOCK)
-            grad[core, at, :] = (e_s[at, lanes] - e_t[at, lanes] * scale).astype(bf16)
-            return 0
-
-        lax.fori_loop(0, PROTOS // BLOCK, body, 0)
-
-    gradients(oc)
-    push(grad.at[oc], grad_mate, mate_send.at[1], mate_recv.at[1], mate)
-    gradients(c)
-
-    def row_product(left, px, right):
-        at = pl.ds(pl.multiple_of(px * SLAB, SLAB), SLAB)
-        return lax.dot_general(left[:, at], right[...], (((0,), (0,)), ((), ())), preferred_element_type=f32)
-
-    for px in range(NX):
-        own[px] = row_product(grad.at[c], px, proto_hat)
-    wait(proto_mate, mate_recv.at[0])
-    wait(grad_mate, mate_recv.at[1])
+    def gradients(core, px):
+        lanes = pl.ds(pl.multiple_of(core * HALF + px * SLAB, SLAB), SLAB)
+        scale = part[pl.ds(core * NX + px, 1), :]
+        grad[core, px] = (e_s[:, lanes] - e_t[:, lanes] * scale).astype(bf16)
+
+    def row_product(left, right):
+        return lax.dot_general(left[...], right[...], (((0,), (0,)), ((), ())), preferred_element_type=f32)
+
     for k in range(NX):
         px = turned(x, k, NX)
-        total = own[px] + row_product(grad_mate, px, proto_mate)
+        gradients(oc, px)
+        push(grad.at[oc, px], grad_mate.at[px], mate_send.at[1], grad_recv.at[px], mate)
+    wait(proto_mate, mate_recv)
+    for k in range(NX):
+        px = turned(x, k, NX)
+        gradients(c, px)
+        own = row_product(grad.at[c, px], proto_hat)
+        wait(grad_mate.at[px], grad_recv.at[px])
+        total = own + row_product(grad_mate.at[px], proto_mate)
         xbuf[px] = total[:, :CUT]
         ubuf[px] = total[:, CUT:].reshape(NU, TILE, D - CUT)
         if k < NX - 1:
@@ -423,13 +415,13 @@
 
     def proto_block(i):
         at = slice(i * 256, (i + 1) * 256)
-        halves = [
-            sum(
-                jnp.dot(grad[core, at, :], gat_s[h, core].reshape(HALF, CUT), preferred_element_type=f32)
-                for core in range(CORES)
-            )
-            for h in range(2)
-        ]
+        halves = [0.0, 0.0]
+        for core in range(CORES):
+            for px in range(0, NX, 2):
+                left = jnp.concatenate([grad[core, px, at, :], grad[core, px + 1, at, :]], axis=1)
+                for h in range(2):
+                    right = gat_s[h, core, px : px + 2].reshape(2 * SLAB, CUT)
+                    halves[h] += jnp.dot(left, right, preferred_element_type=f32)
         step = jnp.concatenate(halves, axis=1)
         inv = proto_inv[at, 0:1]
         unit = proto_ref[at, :].astype(f32) * inv
@@ -511,15 +503,14 @@
             pltpu.VMEM((PROTOS, ROWS), f32),
             pltpu.VMEM((PROTOS, ROWS), f32),
             pltpu.VMEM((PROTOS, LANES), f32),
-            pltpu.VMEM((CORES, PROTOS, HALF), bf16),
+            pltpu.VMEM((CORES, NX, PROTOS, SLAB), bf16),
             pltpu.VMEM((SUMS, TALL, LANES), f32),
             pltpu.VMEM((SUMS, NU * CORES, TALL, LANES), f32),
             pltpu.VMEM((SUMS, TALL, LANES), f32),
             pltpu.VMEM((SUMS, NX * NU, TALL, LANES), f32),
             pltpu.VMEM((TALL, LANES), f32),
-            pltpu.VMEM((NX, SLAB, D), f32),
             pltpu.VMEM((PROTOS, D), bf16),
-            pltpu.VMEM((PROTOS, HALF), bf16),
+            pltpu.VMEM((NX, PROTOS, SLAB), bf16),
             pltpu.VMEM((NX, SLAB, CUT), f32),
             pltpu.VMEM((NX, NU, TILE, D - CUT), f32),
             pltpu.VMEM((NX, SLAB, CUT), f32),
@@ -548,7 +539,8 @@
             dma((SUMS,)),
             dma((SUMS,)),
             dma((2,)),
-            dma((2,)),
+            dma,
+            dma((NX,)),
             dma((2,)),
             dma((2,)),
             dma((3,)),

time: 87.6 us -> 87.8 us (level)
  no operation moved by 1% of the time
where the time goes in v10:
time: 87.8 us; the launch traced here: 87.7 us
  Pallas kernels  85.5 us (97%)
  local copies, waits for them, and re-layouts  1.56 us (2%)
    pallas_call x1, Pallas kernels, on_device(): pl.pallas_call(kernel, out_shape=(jax.ShapeDtypeStruct((OWN, D), f32), ja...  85.5 us

profile of v10, /device:TPU:1, one launch (start us, length us, event | category | flops | bytes accessed | tf_op | source)
XLA Modules:
  0.0 87.7 jit_solution(12727529317071794875)
XLA Ops:
  0.6 85.5 %prototype_head.1 = (f32[2,512]{1,0:T(2,128)S(1)}, f32[512,512]{1,0:T(8,128)S(1)}) custom-call(bf16[2,512]{1,0:T(2,128)(2,1)} %student_hbm.1, bf16[2,512]{1,0:T(2,128)(2,1)} %teacher_hbm.1, bf16[512,512]{1,0:T(8,128)(2,1)} %proto_hbm.1), custom_call_target="tpu_custom_call" | custom-call | tf_op jit(solution)/shard_map/prototype_head/pallas_call | solution.py:485
  86.1 0.6 copy.7
  86.7 1.0 %copy.8 = f32[512,512]{1,0:T(8,128)} copy(f32[512,512]{1,0:T(8,128)S(1)} %get-tuple-element.5) | data formatting | bytes 2097152

commit v11 on v10

--- a/solution.py
+++ b/solution.py
@@ -237,8 +237,8 @@
     spread_hi(gat_t, 1)
     opened_lo(gat_t, 1)
     spread_lo(gat_t, 1)
+    relay(gat_t, 1)
     open_step(gat_s, 0)
-    relay(gat_t, 1)
 
     def exponentials(buf, out, temp, core):
         for k in range(HALF // 256):

time: 87.8 us -> 87.7 us (level)
  no operation moved by 1% of the time
where the time goes in v11:
time: 87.7 us; the launch traced here: 87.6 us
  Pallas kernels  85.4 us (97%)
  local copies, waits for them, and re-layouts  1.56 us (2%)
    pallas_call x1, Pallas kernels, on_device(): pl.pallas_call(kernel, out_shape=(jax.ShapeDtypeStruct((OWN, D), f32), ja...  85.4 us

profile of v11, /device:TPU:1, one launch (start us, length us, event | category | flops | bytes accessed | tf_op | source)
XLA Modules:
  0.0 87.6 jit_solution(3238521455516024151)
XLA Ops:
  0.6 85.4 %prototype_head.1 = (f32[2,512]{1,0:T(2,128)S(1)}, f32[512,512]{1,0:T(8,128)S(1)}) custom-call(bf16[2,512]{1,0:T(2,128)(2,1)} %student_hbm.1, bf16[2,512]{1,0:T(2,128)(2,1)} %teacher_hbm.1, bf16[512,512]{1,0:T(8,128)(2,1)} %proto_hbm.1), custom_call_target="tpu_custom_call" | custom-call | tf_op jit(solution)/shard_map/prototype_head/pallas_call | solution.py:485
  86.0 0.6 copy.7
  86.6 1.0 %copy.8 = f32[512,512]{1,0:T(8,128)} copy(f32[512,512]{1,0:T(8,128)S(1)} %get-tuple-element.5) | data formatting | bytes 2097152

commit v12 on v10

--- a/solution.py
+++ b/solution.py
@@ -274,7 +274,7 @@
             cols[at, :] = jnp.broadcast_to(col, (SWEEP, LANES))
             return acc + folded(e * col)
 
-        return lax.fori_loop(0, PROTOS // SWEEP, body, jnp.zeros((8, ROWS), f32))
+        return lax.fori_loop(0, PROTOS // SWEEP, body, jnp.zeros((8, ROWS), f32), unroll=True)
 
     def near_start(n):
         me = z * CORES + c

time: 87.8 us -> 87.9 us (level)
  no operation moved by 1% of the time
where the time goes in v12:
time: 87.9 us; the launch traced here: 87.8 us
  Pallas kernels  85.6 us (97%)
  local copies, waits for them, and re-layouts  1.56 us (2%)
    pallas_call x1, Pallas kernels, on_device(): pl.pallas_call(kernel, out_shape=(jax.ShapeDtypeStruct((OWN, D), f32), ja...  85.6 us

profile of v12, /device:TPU:1, one launch (start us, length us, event | category | flops | bytes accessed | tf_op | source)
XLA Modules:
  0.0 87.8 jit_solution(13214882634635425812)
XLA Ops:
  0.6 85.6 %prototype_head.1 = (f32[2,512]{1,0:T(2,128)S(1)}, f32[512,512]{1,0:T(8,128)S(1)}) custom-call(bf16[2,512]{1,0:T(2,128)(2,1)} %student_hbm.1, bf16[2,512]{1,0:T(2,128)(2,1)} %teacher_hbm.1, bf16[512,512]{1,0:T(8,128)(2,1)} %proto_hbm.1), custom_call_target="tpu_custom_call" | custom-call | tf_op jit(solution)/shard_map/prototype_head/pallas_call | solution.py:485
  86.2 0.6 copy.7
  86.8 1.0 %copy.8 = f32[512,512]{1,0:T(8,128)} copy(f32[512,512]{1,0:T(8,128)S(1)} %get-tuple-element.5) | data formatting | bytes 2097152
